TPU v7x, 256 devices: a whole 4x4x8 slice. The times are simulated.
256 devices in a mesh: grp: 32 (over z, x_hi, core), blk: 8 (over y, x_lo).
Axes of the slice: x: 4 (x_hi: 2, x_lo: 2; x = x_hi * 2 + x_lo), y: 4, z: 8, core: 2. Of those that a mesh axis runs over, the one named last changes fastest.
Arguments:
- tiles: float32 [1024, 512, 512], P(('grp', 'blk')), as said below
- pairs: int32 [1024, 2], P(('grp', 'blk')), may hold values from 0 to 255, as said below
- direction: float32 [32, 32, 8, 512], P(None, None, 'blk'), may hold values from -6 to 6
Outputs:
- image: float32 [32, 32, 8, 512], P(None, 'grp', 'blk')
Inputs may be any that keep to these rules, and one draw needn't show every extreme that they name: Rows d * 4 to (d + 1) * 4 - 1 of pairs hold pairs (i, j) with i // 8 == d // 8 and j % 8 == d % 8; no unordered pair appears twice; a pair with i < j has i + j even, one with i > j has i + j odd. `tiles`: A tile whose pair has i == j is symmetric.
All inputs are finite; a program needn't handle non-finite values.
Results may differ from a plain program's by a relative error of at most 0.0003.
Values sent between devices are 32-bit elements; how exact they have to be, the bound alone decides.
No kernel may reach another device: no remote copies, remote signals or barrier semaphores. Data moves between devices by JAX's collectives and lax.ppermute only.
A program may use at most 64 MiB of HBM per device.

v0:
```python
import jax
import jax.numpy as jnp
from jax import lax
from jax.sharding import PartitionSpec as P


def shards(tiles, pairs, direction):
    blk_count = lax.axis_size("blk")
    grp_count = lax.axis_size("grp")
    cols = direction.shape[0]
    width = direction.shape[3]
    grp_at = lax.axis_index("grp")
    own_rows = lax.dynamic_slice_in_dim(direction, grp_at, 1, 1)
    row_panel = lax.all_gather(own_rows, "blk", axis=2, tiled=True)[:, 0]
    local_cols = direction[:, :, 0, :]
    rows_at = pairs[:, 0]
    cols_at = pairs[:, 1]
    pick_row = (
        rows_at[:, None] % blk_count == jnp.arange(blk_count, dtype=jnp.int32)[None, :]
    ).astype(jnp.float32)
    pick_col = (
        cols_at[:, None] // blk_count == jnp.arange(grp_count, dtype=jnp.int32)[None, :]
    ).astype(jnp.float32)
    high = lax.Precision.HIGHEST
    left = jnp.einsum("kr,crt->kct", pick_row, row_panel, precision=high)
    right = jnp.einsum("km,cmt->kct", pick_col, local_cols, precision=high)
    row_terms = jnp.einsum("kct,kst->kcs", right, tiles, precision=high)
    mirror = jnp.einsum("kcs,kst->kct", left, tiles, precision=high)
    keep = (rows_at != cols_at).astype(jnp.float32)
    row_part = jnp.einsum("kr,kcs->crs", pick_row, row_terms, precision=high)
    mirror_part = jnp.einsum("km,kct->cmt", pick_col * keep[:, None], mirror, precision=high)
    blk_at = lax.axis_index("blk")
    mark_blk = (jnp.arange(blk_count, dtype=jnp.int32) == blk_at).astype(jnp.float32)
    mark_grp = (jnp.arange(grp_count, dtype=jnp.int32) == grp_at).astype(jnp.float32)
    whole = mirror_part[:, :, None, :] * mark_blk[None, None, :, None]
    whole = whole + row_part[:, None, :, :] * mark_grp[None, :, None, None]
    whole = whole.reshape(cols, grp_count * blk_count, width)
    summed = lax.psum_scatter(whole, ("grp", "blk"), scatter_dimension=1, tiled=True)
    return summed.reshape(cols, 1, 1, width)


def solution(mesh):
    placed = (P(("grp", "blk"), None, None), P(("grp", "blk"), None), P(None, None, "blk", None))
    return jax.shard_map(
        shards, mesh=mesh, in_specs=placed, out_specs=P(None, "grp", "blk", None), check_vma=False
    )
```

profile of v0, /device:TPU:8, one launch (start us, length us, event | category | flops | bytes accessed | tf_op | source)
XLA Modules:
  0.0 1367.7 jit_solution(16403718936029296378)
XLA Ops:
  6.5 0.0 reduce-scatter.2.cloned.1.call-start
  6.5 0.8 fusion.27
  7.3 0.8 fusion.26
  8.1 0.1 mul.60
  8.2 0.1 mul.65
  8.3 0.1 mul.66
  8.4 0.9 constant_dynamic-slice_fusion
  9.2 2.4 fusion.1
  11.6 0.0 copy-start
  11.6 6.2 fusion.8
  17.8 0.6 convolution_bitcast_fusion.1
  18.4 0.3 copy.11
  18.8 29.7 %all_gather.3 = f32[32,1,8,512]{3,0,1,2:T(8,128)S(1)} all-gather(f32[32,1,1,512]{3,0,1,2:T(8,128)S(1)} %copy.14), channel_id=1, replica_groups=mesh['grp'=32,'blk'=8] {'blk'}, dimensions={2}, use_global_device_ids=true | all-gather | bytes 589824 | tf_op jit(solution)/shard_map/all_gather | solution.py:14
  48.4 0.7 fusion.4
  49.1 0.0 copy-done
  49.1 2.5 fusion.11
  51.6 2.0 convolution_bitcast_fusion
  53.6 1.2 copy.8
  54.9 7.7 fusion
  62.5 0.0 reduce-scatter.2.cloned.1.call-update
  62.6 1296.8 %reduce-scatter.2.cloned.1.call-done = f32[32,1,512]{2,0,1:T(8,128)} async-done(((f32[32,256,512]{2,0,1:T(8,128)}), f32[32,1,512]{2,0,1:T(8,128)}) %reduce-scatter.2.cloned.1.call-update) | async-done | bytes 65552 | tf_op jit(solution)/shard_map/reduce_scatter | solution.py:38
  1359.3 1.5 copy.12
  (4 shorter events, 0.0 us)
Async XLA Ops:
  6.5 1352.8 %reduce-scatter.2.cloned.1.call-start = ((), (), s32[]{:S(2)}) async-start(), calls=%async_computation.1 | async-start | bytes 16842752 | tf_op jit(solution)/shard_map/reduce_scatter | solution.py:38
  11.6 37.5 %copy-start = (f32[4,512,512]{2,1,0:T(8,128)S(1)}, f32[4,512,512]{2,1,0:T(8,128)}, u32[]{:S(2)}) copy-start(f32[4,512,512]{2,1,0:T(8,128)} %param.3) | copy-start | bytes 12582916
Sparse Core Ops, SparseCore 0:
  62.7 1296.5 reduce-scatter.1
where the time goes:
time: 1370 us
  waiting for transfers between devices  1300 us (95%)
  blocking collectives  29.7 us (2%)
  matrix products  14.4 us (1%)
    reduce_scatter x1, waiting for transfers between devices, shards(): lax.psum_scatter(whole, ('grp', 'blk'), scatter_dimension=1, tiled=True)  1300 us
    all_gather x1, blocking collectives, shards(): row_panel = lax.all_gather(own_rows, 'blk', axis=2, tiled=True)[:, 0]  29.7 us
  transfers between devices with their start and end apart: 1, of which 1 were waited for; matrix products, arithmetic and copies ran while one was open for 0% of the time, Pallas kernels for 0%

commit v1 on v0

v1 whole, which is shorter than its diff:
```python
import jax
import jax.numpy as jnp
from jax import lax
from jax.experimental import pallas as pl
from jax.experimental.pallas import tpu as pltpu
from jax.sharding import PartitionSpec as P

BLKS = 8
GRPS = 32
ZS = 8
VMEM_BYTES = 40 * 1024 * 1024
VMEM_WHOLE = 62 * 1024 * 1024


def split(x):
    high = x.astype(jnp.bfloat16)
    low = (x - high.astype(jnp.float32)).astype(jnp.bfloat16)
    return high, low


def product(p, tile, contract):
    count = p.shape[0]
    p_parts = jnp.concatenate(split(p), axis=0)
    t_high, t_low = split(tile)
    dims = (((1,), (contract,)), ((), ()))
    first = lax.dot_general(p_parts, t_high, dims, preferred_element_type=jnp.float32)
    second = lax.dot_general(p_parts, t_low, dims, preferred_element_type=jnp.float32)
    both = first + second
    return both[:count] + both[count:]


def rows_kernel(pairs, direction, tiles, out, held, own, picked, tile_sem, pick_sem):
    k_count = tiles.shape[0]
    cols = own.shape[0]
    grp = pairs[0, 0] // BLKS
    own_copy = pltpu.make_async_copy(direction.at[:, grp], own, pick_sem.at[k_count])
    own_copy.start()
    picks, loads = [], []
    for k in range(k_count):
        picks.append(
            pltpu.make_async_copy(direction.at[:, pairs[1, k] // BLKS], picked.at[k], pick_sem.at[k])
        )
        picks[k].start()
        loads.append(pltpu.make_async_copy(tiles.at[k], held.at[k], tile_sem.at[k]))
        loads[k].start()
    own_copy.wait()
    mine = jnp.concatenate([own[:, q, :] for q in range(4)], axis=1)
    for r in range(BLKS):
        out[r, :cols] = mine
        out[r, cols:] = jnp.zeros_like(mine)
    for k in range(k_count):
        picks[k].wait()
        loads[k].wait()
        p = jnp.concatenate([picked[k, :, q, :] for q in range(4)], axis=1)
        r = pairs[0, k] % BLKS
        out[r, cols:] += product(p, held[k], 1)


def mirror_kernel(pairs, got, tiles, send, stay, row_sum):
    k_count = tiles.shape[0]
    cols = row_sum.shape[0]
    x_mine = (pairs[0, 0] // BLKS) // 2 % 2
    total = got[0, cols:]
    for b in range(1, BLKS):
        total = total + got[b, cols:]
    row_sum[...] = total
    for k in range(k_count):
        i, j = pairs[0, k], pairs[1, k]
        m = j // BLKS
        value = product(got[i % BLKS, :cols], tiles[k], 0)
        value = jnp.where(i != j, value, 0.0)
        stay[k] = value
        send[pl.ds(k * cols, cols)] = value
        place = jnp.where(m // 2 % 2 != x_mine, m // 4 * 2 + m % 2, -1).astype(jnp.float32)
        send[k_count * cols:, pl.ds(k * 128, 128)] = jnp.full((8, 128), place, jnp.float32)


def place_kernel(pairs, stay, came, send, keep):
    k_count, cols, width = stay.shape
    grp = pairs[0, 0] // BLKS
    core = grp % 2
    x_mine = grp // 2 % 2
    send[...] = jnp.zeros_like(send)
    keep[...] = jnp.zeros_like(keep)

    def add(place, value):
        z = place // 2

        @pl.when((place >= 0) & (place % 2 == core))
        def _():
            keep[z] += value

        @pl.when((place >= 0) & (place % 2 != core))
        def _():
            send[z] += value

    for k in range(k_count):
        m = pairs[1, k] // BLKS
        add(jnp.where(m // 2 % 2 == x_mine, m // 4 * 2 + m % 2, -1), stay[k])
        place = jnp.max(came[k_count * cols:, pl.ds(k * 128, 128)]).astype(jnp.int32)
        add(place, came[pl.ds(k * cols, cols)])


def shards(tiles, pairs, direction):
    k_count, width, _ = tiles.shape
    cols = direction.shape[0]
    f32 = jnp.float32
    smem = pl.BlockSpec(memory_space=pltpu.SMEM)
    vmem = pl.BlockSpec(memory_space=pltpu.VMEM)
    hbm = pl.BlockSpec(memory_space=pltpu.HBM)
    params = pltpu.CompilerParams(vmem_limit_bytes=VMEM_BYTES)
    pairs = pairs.T
    lanes = direction.reshape(cols, GRPS, 4, 128)
    first = pl.pallas_call(
        rows_kernel,
        out_shape=jax.ShapeDtypeStruct((BLKS, 2 * cols, width), f32),
        in_specs=[smem, hbm, hbm],
        out_specs=vmem,
        scratch_shapes=[
            pltpu.VMEM((k_count, width, width), f32),
            pltpu.VMEM((cols, 4, 128), f32),
            pltpu.VMEM((k_count, cols, 4, 128), f32),
            pltpu.SemaphoreType.DMA((k_count,)),
            pltpu.SemaphoreType.DMA((k_count + 1,)),
        ],
        compiler_params=pltpu.CompilerParams(vmem_limit_bytes=VMEM_WHOLE),
        name="rows",
    )(pairs, lanes, tiles)
    got = lax.all_to_all(first, "blk", 0, 0, tiled=True)
    send, stay, row_sum = pl.pallas_call(
        mirror_kernel,
        out_shape=[
            jax.ShapeDtypeStruct((k_count * cols + 8, width), f32),
            jax.ShapeDtypeStruct((k_count, cols, width), f32),
            jax.ShapeDtypeStruct((cols, width), f32),
        ],
        in_specs=[smem, vmem, vmem],
        out_specs=[vmem, vmem, vmem],
        compiler_params=params,
        name="mirror",
    )(pairs, got, tiles)
    came = lax.ppermute(send, "grp", [(g, g ^ 2) for g in range(GRPS)])
    send, keep = pl.pallas_call(
        place_kernel,
        out_shape=[jax.ShapeDtypeStruct((ZS, cols, width), f32)] * 2,
        in_specs=[smem, vmem, vmem],
        out_specs=[vmem, vmem],
        compiler_params=params,
        name="place",
    )(pairs, stay, came)
    came = lax.ppermute(send, "grp", [(g, g ^ 1) for g in range(GRPS)])
    part = keep + came
    along_z = [[z * 4 + q for z in range(ZS)] for q in range(4)]
    parts = lax.all_to_all(part, "grp", 0, 0, tiled=True, axis_index_groups=along_z)
    return (jnp.sum(parts, axis=0) + row_sum).reshape(cols, 1, 1, width)


def solution(mesh):
    placed = (P(("grp", "blk"), None, None), P(("grp", "blk"), None), P(None, None, "blk", None))
    return jax.shard_map(
        shards, mesh=mesh, in_specs=placed, out_specs=P(None, "grp", "blk", None), check_vma=False
    )
```

time: 1370 us -> 68.9 us (0.05)
  the two profiles are of different devices: /device:TPU:8 before, /device:TPU:1 now
where the time goes in v1:
time: 68.9 us; the launch traced here: 68.6 us
  blocking collectives  45.6 us (66%)
  Pallas kernels  7.71 us (11%)
  waiting for transfers between devices  6.89 us (10%)
  starting transfers between devices  5.41 us (8%)
  local copies, waits for them, and re-layouts  2.89 us (4%)
    all_to_all x1, blocking collectives, shards(): lax.all_to_all(part, 'grp', 0, 0, tiled=True, axis_index_groups=along_z)  24.7 us
    all_to_all x1, blocking collectives, shards(): got = lax.all_to_all(first, 'blk', 0, 0, tiled=True)  20.9 us
    ppermute x1, waiting for transfers between devices, shards(): came = lax.ppermute(send, 'grp', [(g, g ^ 2) for g in range(GRPS)])  5.35 us
    pallas_call x1, Pallas kernels, shards(): pl.pallas_call(rows_kernel, out_shape=jax.ShapeDtypeStruct((BLKS, 2 * col...  4.95 us
    ppermute x1, starting transfers between devices, shards(): came = lax.ppermute(send, 'grp', [(g, g ^ 1) for g in range(GRPS)])  2.88 us
    ppermute x1, starting transfers between devices, shards(): came = lax.ppermute(send, 'grp', [(g, g ^ 2) for g in range(GRPS)])  2.53 us
    unnamed x4, local copies, waits for them, and re-layouts  2.19 us
    ppermute x1, waiting for transfers between devices, shards(): came = lax.ppermute(send, 'grp', [(g, g ^ 1) for g in range(GRPS)])  1.54 us
  transfers between devices with their start and end apart: 2, of which 2 were waited for; matrix products, arithmetic and copies ran while one was open for 0% of the time, Pallas kernels for 0%

profile of v1, /device:TPU:1, one launch (start us, length us, event | category | flops | bytes accessed | tf_op | source)
XLA Modules:
  0.0 68.6 jit_solution(14773019762241815724)
XLA Ops:
  0.0 0.0 copy-start.1
  0.0 4.9 %rows.1 = f32[8,64,512]{2,1,0:T(8,128)} custom-call(s32[2,4]{1,0:T(2,128)} %bitcast.4, f32[32,32,4,128]{3,2,1,0:T(4,128)} %bitcast.7, f32[4,512,512]{2,1,0:T(8,128)} %tiles.3), custom_call_target="tpu_custom_call" | custom-call | tf_op jit(solution)/shard_map/rows/pallas_call | solution.py:114
  5.0 20.9 %all_to_all.10.got = f32[8,64,512]{2,1,0:T(8,128)S(1)} all-to-all(f32[8,64,512]{2,1,0:T(8,128)} %rows.1), channel_id=1, replica_groups=mesh['grp'=32,'blk'=8] {'blk'}, dimensions={0} | all-to-all | bytes 2097152 | tf_op jit(solution)/shard_map/all_to_all | solution.py:129
  25.8 0.0 copy-done.1
  25.8 0.0 copy-start
  25.8 2.2 %copy-done = f32[4,512,512]{2,1,0:T(8,128)S(1)} copy-done((f32[4,512,512]{2,1,0:T(8,128)S(1)}, f32[4,512,512]{2,1,0:T(8,128)}, u32[]{:S(2)}) %copy-start) | copy-done | bytes 4194328
  28.0 1.5 %mirror.1 = (f32[136,512]{1,0:T(8,128)S(1)}, f32[4,32,512]{2,1,0:T(8,128)S(1)}, f32[32,512]{1,0:T(8,128)S(1)}) custom-call(s32[2,4]{1,0:T(2,128)S(1)} %bitcast.5, f32[8,64,512]{2,1,0:T(8,128)S(1)} %all_to_all.10.got, f32[4,512,512]{2,1,0:T(8,128)S(1)} %copy-done), custom_call_target="tpu_custom_call" | custom-call | tf_op jit(solution)/shard_map/mirror/pallas_call | solution.py:130
  29.5 2.5 %collective-permute-start = (f32[136,512]{1,0:T(8,128)S(1)}, f32[136,512]{1,0:T(8,128)S(1)}, u32[]{:S(2)}, u32[]{:S(2)}) collective-permute-start(f32[136,512]{1,0:T(8,128)S(1)} %get-tuple-element.11), channel_id=1, source_target_pairs={{0,16},{8,24},{16,0},{24,8},{32,48},{40,56},{48,32},{56,40},{64,80... | collective-permute-start | bytes 835592 | tf_op jit(solution)/shard_map/ppermute | solution.py:142
  32.1 5.3 %collective-permute-done.came = f32[136,512]{1,0:T(8,128)S(1)} collective-permute-done((f32[136,512]{1,0:T(8,128)S(1)}, f32[136,512]{1,0:T(8,128)S(1)}, u32[]{:S(2)}, u32[]{:S(2)}) %collective-permute-start) | collective-permute-done | bytes 278560 | tf_op jit(solution)/shard_map/ppermute | solution.py:142
  37.4 1.3 %place.1 = (f32[8,32,512]{2,1,0:T(8,128)S(1)}, f32[8,32,512]{2,1,0:T(8,128)S(1)}) custom-call(s32[2,4]{1,0:T(2,128)S(1)} %bitcast.6, f32[4,32,512]{2,1,0:T(8,128)S(1)} %get-tuple-element.10.stay, f32[136,512]{1,0:T(8,128)S(1)} %collective-permute-done.came), custom_call_target="tpu_custom_call" | custom-call | tf_op jit(solution)/shard_map/place/pallas_call | solution.py:143
  38.7 2.9 %collective-permute-start.1 = (f32[8,32,512]{2,1,0:T(8,128)S(1)}, f32[8,32,512]{2,1,0:T(8,128)S(1)}, u32[]{:S(2)}, u32[]{:S(2)}) collective-permute-start(f32[8,32,512]{2,1,0:T(8,128)S(1)} %get-tuple-element.13), channel_id=1, source_target_pairs={{0,8},{8,0},{16,24},{24,16},{32,40},{40,32},{48,56},{56,48},{64,72... | collective-permute-start | bytes 1572872 | tf_op jit(solution)/shard_map/ppermute | solution.py:151
  41.6 1.5 %collective-permute-done.1 = f32[8,32,512]{2,1,0:T(8,128)S(1)} collective-permute-done((f32[8,32,512]{2,1,0:T(8,128)S(1)}, f32[8,32,512]{2,1,0:T(8,128)S(1)}, u32[]{:S(2)}, u32[]{:S(2)}) %collective-permute-start.1) | collective-permute-done | bytes 524320 | tf_op jit(solution)/shard_map/ppermute | solution.py:151
  43.1 0.1 add.6
  43.2 24.7 %all_to_all.11 = f32[8,32,512]{2,1,0:T(8,128)S(1)} all-to-all(f32[8,32,512]{2,1,0:T(8,128)S(1)} %add.6), channel_id=1, replica_groups={{0,32,64,96,128,160,192,224},{8,40,72,104,136,168,200,232},{16,48,80,11..., dimensions={0} | all-to-all | bytes 1048576 | tf_op jit(solution)/shard_map/all_to_all | solution.py:154
  67.9 0.7 %copy.4 = f32[32,1,1,512]{3,2,1,0:T(1,128)} copy(f32[32,1,1,512]{3,0,2,1:T(8,128)S(1)} %add_bitcast_fusion) | data formatting | bytes 131072 | tf_op jit(solution)/shard_map/reshape | solution.py:155
  (2 shorter events, 0.0 us)
Async XLA Ops:
  0.0 25.8 %copy-start.1 = (s32[4,2]{0,1:T(2,128)S(1)}, s32[4,2]{0,1:T(2,128)}, u32[]{:S(2)}) copy-start(s32[4,2]{0,1:T(2,128)} %param.4) | copy-start | bytes 100
  25.8 2.2 %copy-start = (f32[4,512,512]{2,1,0:T(8,128)S(1)}, f32[4,512,512]{2,1,0:T(8,128)}, u32[]{:S(2)}) copy-start(f32[4,512,512]{2,1,0:T(8,128)} %tiles.3) | copy-start | bytes 12582916
  29.5 7.9 %collective-permute-start = (f32[136,512]{1,0:T(8,128)S(1)}, f32[136,512]{1,0:T(8,128)S(1)}, u32[]{:S(2)}, u32[]{:S(2)}) collective-permute-start(f32[136,512]{1,0:T(8,128)S(1)} %get-tuple-element.11), channel_id=1, source_target_pairs={{0,16},{8,24},{16,0},{24,8},{32,48},{40,56},{48,32},{56,40},{64,80... | collective-permute-start | bytes 835592 | tf_op jit(solution)/shard_map/ppermute | solution.py:142
  38.7 4.4 %collective-permute-start.1 = (f32[8,32,512]{2,1,0:T(8,128)S(1)}, f32[8,32,512]{2,1,0:T(8,128)S(1)}, u32[]{:S(2)}, u32[]{:S(2)}) collective-permute-start(f32[8,32,512]{2,1,0:T(8,128)S(1)} %get-tuple-element.13), channel_id=1, source_target_pairs={{0,8},{8,0},{16,24},{24,16},{32,40},{40,32},{48,56},{56,48},{64,72... | collective-permute-start | bytes 1572872 | tf_op jit(solution)/shard_map/ppermute | solution.py:151

commit v2 on v1

v2 whole, which is shorter than its diff:
```python
import jax
import jax.numpy as jnp
from jax import lax
from jax.experimental import pallas as pl
from jax.experimental.pallas import tpu as pltpu
from jax.sharding import PartitionSpec as P

BLKS = 8
GRPS = 32
ZS = 8
YS = 4
VMEM_BYTES = 32 * 1024 * 1024


def split(x):
    high = x.astype(jnp.bfloat16)
    low = (x - high.astype(jnp.float32)).astype(jnp.bfloat16)
    return high, low


def product(p, tile, contract):
    count = p.shape[0]
    p_parts = jnp.concatenate(split(p), axis=0)
    t_high, t_low = split(tile)
    dims = (((1,), (contract,)), ((), ()))
    first = lax.dot_general(p_parts, t_high, dims, preferred_element_type=jnp.float32)
    second = lax.dot_general(p_parts, t_low, dims, preferred_element_type=jnp.float32)
    both = first + second
    return both[:count] + both[count:]


def joined(ref):
    return jnp.concatenate([ref[:, q, :] for q in range(4)], axis=1)


def own_kernel(direction, out, own, sem):
    copy = pltpu.make_async_copy(direction.at[:, lax.axis_index("grp")], own, sem)
    copy.start()
    copy.wait()
    mine = joined(own)
    for r in range(BLKS):
        out[r] = mine


def rows_kernel(pairs, direction, tiles, out, kept, rest, picked, tile_sem, pick_sem):
    k_count = tiles.shape[0]
    held = [kept.at[k] for k in range(kept.shape[0])] + [rest.at[k] for k in range(rest.shape[0])]
    picks, loads = [], []
    for k in range(k_count):
        picks.append(
            pltpu.make_async_copy(direction.at[:, pairs[1, k] // BLKS], picked.at[k], pick_sem.at[k])
        )
        picks[k].start()
        loads.append(pltpu.make_async_copy(tiles.at[k], held[k], tile_sem.at[k]))
        loads[k].start()
    out[...] = jnp.zeros_like(out)
    for k in range(k_count):
        picks[k].wait()
        loads[k].wait()
        r, b = pairs[0, k] % BLKS, pairs[1, k] % BLKS
        out[(r + b) % 2, (r // 2 + YS - b // 2) % YS] += product(joined(picked.at[k]), held[k][...], 1)


def mirror_kernel(pairs, got, kept, tiles, out, rest, tile_sem):
    k_count = tiles.shape[0]
    cols = got.shape[1]
    near = kept.shape[0]
    loads = []
    for k in range(near, k_count):
        loads.append(pltpu.make_async_copy(tiles.at[k], rest.at[k - near], tile_sem.at[k - near]))
        loads[-1].start()
    for k in range(k_count):
        if k >= near:
            loads[k - near].wait()
        tile = kept[k] if k < near else rest[k - near]
        i, j = pairs[0, k], pairs[1, k]
        out[pl.ds(k * cols, cols)] = product(got[i % BLKS], tile, 0)
        place = jnp.where(i != j, j // BLKS, -1).astype(jnp.float32)
        out[k_count * cols:, pl.ds(k * 128, 128)] = jnp.full((8, 128), place, jnp.float32)


def place_kernel(pairs, *refs):
    *parts, out = refs
    cols, width = out.shape[1:]
    k_count = width // 128
    mine = pairs[0, 0] // BLKS % 4
    groups = [jnp.where(pairs[0, k] != pairs[1, k], pairs[1, k] // BLKS, -1) for k in range(k_count)]
    for part in parts[1:]:
        for k in range(k_count):
            groups.append(part[pl.ds(k_count * cols, 1), pl.ds(k * 128, 128)][0, 0].astype(jnp.int32))
    out[...] = jnp.zeros_like(out)
    for at, part in enumerate(parts):
        for k in range(k_count):
            m = groups[at * k_count + k]

            @pl.when((m >= 0) & (m % 4 == mine))
            def _():
                out[m // 4] += part[pl.ds(k * cols, cols)]


def shards(tiles, pairs, direction):
    k_count, width, _ = tiles.shape
    cols = direction.shape[0]
    f32 = jnp.float32
    smem = pl.BlockSpec(memory_space=pltpu.SMEM)
    vmem = pl.BlockSpec(memory_space=pltpu.VMEM)
    hbm = pl.BlockSpec(memory_space=pltpu.HBM)
    params = pltpu.CompilerParams(vmem_limit_bytes=VMEM_BYTES)
    pairs = pairs.T
    lanes = pltpu.with_memory_space_constraint(direction.reshape(cols, GRPS, 4, 128), pltpu.HBM)
    own = pl.pallas_call(
        own_kernel,
        out_shape=jax.ShapeDtypeStruct((BLKS, cols, width), f32),
        in_specs=[hbm],
        out_specs=vmem,
        scratch_shapes=[pltpu.VMEM((cols, 4, 128), f32), pltpu.SemaphoreType.DMA],
        compiler_params=params,
        name="own",
    )(lanes)
    got = lax.all_to_all(own, "blk", 0, 0, tiled=True)
    near = k_count // 2
    tiles = pltpu.with_memory_space_constraint(tiles, pltpu.HBM)
    rows, kept = pl.pallas_call(
        rows_kernel,
        out_shape=[
            jax.ShapeDtypeStruct((2, YS, cols, width), f32),
            jax.ShapeDtypeStruct((near, width, width), f32),
        ],
        in_specs=[smem, hbm, hbm],
        out_specs=[vmem, vmem],
        scratch_shapes=[
            pltpu.VMEM((k_count - near, width, width), f32),
            pltpu.VMEM((k_count, cols, 4, 128), f32),
            pltpu.SemaphoreType.DMA((k_count,)),
            pltpu.SemaphoreType.DMA((k_count,)),
        ],
        compiler_params=params,
        cost_estimate=pl.CostEstimate(flops=600_000_000, bytes_accessed=10_000_000, transcendentals=0),
        name="rows",
    )(pairs, lanes, tiles)
    rows = rows[0] + lax.ppermute(rows[1], "blk", [(b, b ^ 1) for b in range(BLKS)])
    terms = pl.pallas_call(
        mirror_kernel,
        out_shape=jax.ShapeDtypeStruct((k_count * cols + 8, width), f32),
        in_specs=[smem, vmem, vmem, hbm],
        out_specs=vmem,
        scratch_shapes=[
            pltpu.VMEM((k_count - near, width, width), f32),
            pltpu.SemaphoreType.DMA((k_count - near,)),
        ],
        compiler_params=params,
        name="mirror",
    )(pairs, got, kept, tiles)
    over_x = lax.ppermute(terms, "grp", [(g, g ^ 2) for g in range(GRPS)])
    over_core = lax.ppermute(terms, "grp", [(g, g ^ 1) for g in range(GRPS)])
    over_both = lax.ppermute(over_x, "grp", [(g, g ^ 1) for g in range(GRPS)])
    part = pl.pallas_call(
        place_kernel,
        out_shape=jax.ShapeDtypeStruct((ZS, cols, width), f32),
        in_specs=[smem, vmem, vmem, vmem, vmem],
        out_specs=vmem,
        compiler_params=params,
        name="place",
    )(pairs, terms, over_core, over_x, over_both)
    along_z = [[z * 4 + q for z in range(ZS)] for q in range(4)]
    parts = lax.all_to_all(part, "grp", 0, 0, tiled=True, axis_index_groups=along_z)
    total = rows[0]
    for step in range(1, YS):
        total = total + lax.ppermute(rows[step], "blk", [(b, (b + 2 * step) % BLKS) for b in range(BLKS)])
    total = total + jnp.sum(parts, axis=0)
    return total.reshape(cols, 1, 1, width)


def solution(mesh):
    placed = (P(("grp", "blk"), None, None), P(("grp", "blk"), None), P(None, None, "blk", None))
    return jax.shard_map(
        shards, mesh=mesh, in_specs=placed, out_specs=P(None, "grp", "blk", None), check_vma=False
    )
```

time: 68.9 us -> 60.1 us (0.87)
  blocking collectives: 45.6 us -> 0 us
  starting transfers between devices: 5.41 us -> 24.7 us
  waiting for transfers between devices: 6.89 us -> 24.4 us
  local copies, waits for them, and re-layouts: 2.89 us -> 0.73 us
  Pallas kernels: 7.71 us -> 9.76 us
    all_to_all x2 -> x0, blocking collectives: 45.6 us -> none  [the longest x1 24.7 us: shards(): lax.all_to_all(part, 'grp', 0, 0, tiled=True, axis_index_groups=along_z)]
    all_to_all x0 -> x2, starting transfers between devices: none -> 14.2 us  [the longest x1 8.2 us: shards(): lax.all_to_all(part, 'grp', 0, 0, tiled=True, axis_index_groups=along_z)]
    all_to_all x0 -> x2, waiting for transfers between devices: none -> 13.1 us  [the longest x1 7.79 us: shards(): lax.all_to_all(part, 'grp', 0, 0, tiled=True, axis_index_groups=along_z)]
    ppermute x2 -> x7, starting transfers between devices: 5.41 us -> 10.6 us  [the longest x1 2.79 us: shards(): over_both = lax.ppermute(over_x, 'grp', [(g, g ^ 1) for g in range(GRPS)])]
    ppermute x2 -> x7, waiting for transfers between devices: 6.89 us -> 11.4 us  [the longest x1 6.99 us: shards(): lax.ppermute(rows[1], 'blk', [(b, b ^ 1) for b in range(BLKS)])]
    unnamed x4 -> x2, local copies, waits for them, and re-layouts: 2.19 us -> 0.01 us
    pallas_call x3 -> x4, Pallas kernels: 7.71 us -> 9.76 us  [the longest x1 3.9 us: shards(): pl.pallas_call(rows_kernel, out_shape=[jax.ShapeDtypeStruct((2, YS, cols,...]
  transfers between devices with their start and end apart: 2 -> 9, of which waited for: 2 -> 5; matrix products, arithmetic and copies ran while one was open for 0% -> 0% of each run, Pallas kernels for 0% -> 7%
where the time goes in v2:
time: 60.1 us; the launch traced here: 59.8 us
  starting transfers between devices  24.7 us (41%)
  waiting for transfers between devices  24.4 us (41%)
  Pallas kernels  9.76 us (16%)
  local copies, waits for them, and re-layouts  0.73 us (1%)
    all_to_all x1, starting transfers between devices, shards(): lax.all_to_all(part, 'grp', 0, 0, tiled=True, axis_index_groups=along_z)  8.2 us
    all_to_all x1, waiting for transfers between devices, shards(): lax.all_to_all(part, 'grp', 0, 0, tiled=True, axis_index_groups=along_z)  7.79 us
    ppermute x1, waiting for transfers between devices, shards(): lax.ppermute(rows[1], 'blk', [(b, b ^ 1) for b in range(BLKS)])  6.99 us
    all_to_all x1, starting transfers between devices, shards(): got = lax.all_to_all(own, 'blk', 0, 0, tiled=True)  5.96 us
    all_to_all x1, waiting for transfers between devices, shards(): got = lax.all_to_all(own, 'blk', 0, 0, tiled=True)  5.26 us
    pallas_call x1, Pallas kernels, shards(): pl.pallas_call(rows_kernel, out_shape=[jax.ShapeDtypeStruct((2, YS, cols,...  3.9 us
    ppermute x1, waiting for transfers between devices, shards(): over_x = lax.ppermute(terms, 'grp', [(g, g ^ 2) for g in range(GRPS)])  3.19 us
    ppermute x1, starting transfers between devices, shards(): over_both = lax.ppermute(over_x, 'grp', [(g, g ^ 1) for g in range(GRPS)])  2.79 us
  transfers between devices with their start and end apart: 9, of which 5 were waited for; matrix products, arithmetic and copies ran while one was open for 0% of the time, Pallas kernels for 7%

profile of v2, /device:TPU:1, one launch (start us, length us, event | category | flops | bytes accessed | tf_op | source)
XLA Modules:
  0.0 59.8 jit_solution(12735603028069780810)
XLA Ops:
  0.0 1.7 %own.1 = f32[8,32,512]{2,1,0:T(8,128)} custom-call(f32[32,32,4,128]{3,2,1,0:T(4,128)} %bitcast.29), custom_call_target="tpu_custom_call" | custom-call | tf_op jit(solution)/shard_map/own/pallas_call | solution.py:111
  1.7 6.0 %all-to-all-start = ((f32[8,32,512]{2,1,0:T(8,128)}), f32[8,32,512]{2,1,0:T(8,128)S(1)}, u32[]{:S(2)}, u32[]{:S(2)}) async-start(f32[8,32,512]{2,1,0:T(8,128)} %own.1), calls=%async_computation | async-start | bytes 1048576 | tf_op jit(solution)/shard_map/all_to_all | solution.py:120
  7.7 0.0 copy-done
  7.7 3.9 %rows.1 = (f32[2,4,32,512]{3,2,1,0:T(8,128)S(1)}, f32[2,512,512]{2,1,0:T(8,128)S(1)}) custom-call(s32[2,4]{1,0:T(2,128)S(1)} %bitcast.26, f32[32,32,4,128]{3,2,1,0:T(4,128)} %bitcast.30, f32[4,512,512]{2,1,0:T(8,128)} %tiles.3), custom_call_target="tpu_custom_call" | custom-call | flops 600000000 | bytes 10000000 | tf_op jit(solution)/shard_map/rows/pallas_call | solution.py:123
  11.6 5.3 %all-to-all-done.got = f32[8,32,512]{2,1,0:T(8,128)S(1)} async-done(((f32[8,32,512]{2,1,0:T(8,128)}), f32[8,32,512]{2,1,0:T(8,128)S(1)}, u32[]{:S(2)}, u32[]{:S(2)}) %all-to-all-start) | async-done | bytes 524320 | tf_op jit(solution)/shard_map/all_to_all | solution.py:120
  16.8 2.5 %mirror.1.refs_0_ = f32[136,512]{1,0:T(8,128)S(1)} custom-call(s32[2,4]{1,0:T(2,128)S(1)} %bitcast.27, f32[8,32,512]{2,1,0:T(8,128)S(1)} %all-to-all-done.got, f32[2,512,512]{2,1,0:T(8,128)S(1)} %get-tuple-element.8.kept, f32[4,512,512]{2,1,0:T(8,128)} %tiles.3), custom_call_target="tpu_custom_call" | custom-call | tf_op jit(solution)/shard_map/mirror/pallas_call | solution.py:142
  19.4 2.5 %collective-permute-start.5 = (f32[136,512]{1,0:T(8,128)S(1)}, f32[136,512]{1,0:T(8,128)S(1)}, u32[]{:S(2)}, u32[]{:S(2)}) collective-permute-start(f32[136,512]{1,0:T(8,128)S(1)} %mirror.1.refs_0_), channel_id=1, source_target_pairs={{0,16},{8,24},{16,0},{24,8},{32,48},{40,56},{48,32},{56,40},{64,80... | collective-permute-start | bytes 835592 | tf_op jit(solution)/shard_map/ppermute | solution.py:154
  21.9 2.1 %collective-permute-start.4 = (f32[136,512]{1,0:T(8,128)S(1)}, f32[136,512]{1,0:T(8,128)S(1)}, u32[]{:S(2)}, u32[]{:S(2)}) collective-permute-start(f32[136,512]{1,0:T(8,128)S(1)} %mirror.1.refs_0_), channel_id=1, source_target_pairs={{0,8},{8,0},{16,24},{24,16},{32,40},{40,32},{48,56},{56,48},{64,72... | collective-permute-start | bytes 835592 | tf_op jit(solution)/shard_map/ppermute | solution.py:155
  24.1 3.2 %collective-permute-done.5.refs_2_ = f32[136,512]{1,0:T(8,128)S(1)} collective-permute-done((f32[136,512]{1,0:T(8,128)S(1)}, f32[136,512]{1,0:T(8,128)S(1)}, u32[]{:S(2)}, u32[]{:S(2)}) %collective-permute-start.5) | collective-permute-done | bytes 278560 | tf_op jit(solution)/shard_map/ppermute | solution.py:154
  27.3 2.8 %collective-permute-start.6 = (f32[136,512]{1,0:T(8,128)S(1)}, f32[136,512]{1,0:T(8,128)S(1)}, u32[]{:S(2)}, u32[]{:S(2)}) collective-permute-start(f32[136,512]{1,0:T(8,128)S(1)} %collective-permute-done.5.refs_2_), channel_id=1, source_target_pairs={{0,8},{8,0},{16,24},{24,16},{32,40},{40,32},{48,56},{56,48},{64,72... | collective-permute-start | bytes 835592 | tf_op jit(solution)/shard_map/ppermute | solution.py:156
  30.0 0.0 collective-permute-done.4.refs_1_
  30.1 1.2 %collective-permute-done.6.refs_3_ = f32[136,512]{1,0:T(8,128)S(1)} collective-permute-done((f32[136,512]{1,0:T(8,128)S(1)}, f32[136,512]{1,0:T(8,128)S(1)}, u32[]{:S(2)}, u32[]{:S(2)}) %collective-permute-start.6) | collective-permute-done | bytes 278560 | tf_op jit(solution)/shard_map/ppermute | solution.py:156
  31.2 1.6 %place.1 = f32[8,32,512]{2,1,0:T(8,128)} custom-call(s32[2,4]{1,0:T(2,128)S(1)} %bitcast.28, f32[136,512]{1,0:T(8,128)S(1)} %mirror.1.refs_0_, f32[136,512]{1,0:T(8,128)S(1)} %collective-permute-done.4.refs_1_, f32[136,512]{1,0:T(8,128)S(1)} %collective-permute-done.5.refs_2_, f32[136,512]{1,0:T(8,128)S(1)} %collective-permute-done.6.refs_3_), custom_call_target="tpu_custom_call" | custom-call | tf_op jit(solution)/shard_map/place/pallas_call | solution.py:157
  32.9 8.2 %all-to-all-start.1 = ((f32[8,32,512]{2,1,0:T(8,128)}), f32[8,32,512]{2,1,0:T(8,128)S(1)}, u32[]{:S(2)}, u32[]{:S(2)}) async-start(f32[8,32,512]{2,1,0:T(8,128)} %place.1), calls=%async_computation.1 | async-start | bytes 1048576 | tf_op jit(solution)/shard_map/all_to_all | solution.py:166
  41.1 0.3 collective-permute-start
  41.4 7.0 %collective-permute-done = f32[4,32,512]{2,1,0:T(8,128)S(1)} collective-permute-done((f32[4,32,512]{2,1,0:T(8,128)S(1)}, f32[4,32,512]{2,1,0:T(8,128)S(1)}, u32[]{:S(2)}, u32[]{:S(2)}) %collective-permute-start) | collective-permute-done | bytes 262176 | tf_op jit(solution)/shard_map/ppermute | solution.py:141
  48.5 0.1 collective-permute-start.1
  48.6 2.7 %collective-permute-start.3 = (f32[32,512]{1,0:T(8,128)S(1)}, f32[32,512]{1,0:T(8,128)S(1)}, u32[]{:S(2)}, u32[]{:S(2)}) collective-permute-start(f32[32,512]{1,0:T(8,128)S(1)} %get-tuple-element.10), channel_id=1, source_target_pairs={{0,6},{1,7},{2,0},{3,1},{4,2},{5,3},{6,4},{7,5},{8,14},{9,15},{10,... | collective-permute-start | bytes 196616 | tf_op jit(solution)/shard_map/ppermute | solution.py:169
  51.2 0.0 collective-permute-start.2
  51.2 7.8 %all-to-all-done.1 = f32[8,32,512]{2,1,0:T(8,128)S(1)} async-done(((f32[8,32,512]{2,1,0:T(8,128)}), f32[8,32,512]{2,1,0:T(8,128)S(1)}, u32[]{:S(2)}, u32[]{:S(2)}) %all-to-all-start.1) | async-done | bytes 524320 | tf_op jit(solution)/shard_map/all_to_all | solution.py:166
  59.1 0.0 collective-permute-done.1
  59.1 0.0 collective-permute-done.3
  59.1 0.0 collective-permute-done.2
  59.1 0.7 %copy.4 = f32[32,1,1,512]{3,2,1,0:T(1,128)} copy(f32[32,1,1,512]{3,0,2,1:T(8,128)S(1)} %fusion.4) | data formatting | bytes 131072 | tf_op jit(solution)/shard_map/reshape | solution.py:171
  (6 shorter events, 0.1 us)
Async XLA Ops:
  0.0 7.7 %copy-start = (s32[4,2]{0,1:T(2,128)S(1)}, s32[4,2]{0,1:T(2,128)}, u32[]{:S(2)}) copy-start(s32[4,2]{0,1:T(2,128)} %param.4) | copy-start | bytes 100
  1.7 15.1 %all-to-all-start = ((f32[8,32,512]{2,1,0:T(8,128)}), f32[8,32,512]{2,1,0:T(8,128)S(1)}, u32[]{:S(2)}, u32[]{:S(2)}) async-start(f32[8,32,512]{2,1,0:T(8,128)} %own.1), calls=%async_computation | async-start | bytes 1048576 | tf_op jit(solution)/shard_map/all_to_all | solution.py:120
  19.4 7.9 %collective-permute-start.5 = (f32[136,512]{1,0:T(8,128)S(1)}, f32[136,512]{1,0:T(8,128)S(1)}, u32[]{:S(2)}, u32[]{:S(2)}) collective-permute-start(f32[136,512]{1,0:T(8,128)S(1)} %mirror.1.refs_0_), channel_id=1, source_target_pairs={{0,16},{8,24},{16,0},{24,8},{32,48},{40,56},{48,32},{56,40},{64,80... | collective-permute-start | bytes 835592 | tf_op jit(solution)/shard_map/ppermute | solution.py:154
  21.9 8.1 %collective-permute-start.4 = (f32[136,512]{1,0:T(8,128)S(1)}, f32[136,512]{1,0:T(8,128)S(1)}, u32[]{:S(2)}, u32[]{:S(2)}) collective-permute-start(f32[136,512]{1,0:T(8,128)S(1)} %mirror.1.refs_0_), channel_id=1, source_target_pairs={{0,8},{8,0},{16,24},{24,16},{32,40},{40,32},{48,56},{56,48},{64,72... | collective-permute-start | bytes 835592 | tf_op jit(solution)/shard_map/ppermute | solution.py:155
  27.3 4.0 %collective-permute-start.6 = (f32[136,512]{1,0:T(8,128)S(1)}, f32[136,512]{1,0:T(8,128)S(1)}, u32[]{:S(2)}, u32[]{:S(2)}) collective-permute-start(f32[136,512]{1,0:T(8,128)S(1)} %collective-permute-done.5.refs_2_), channel_id=1, source_target_pairs={{0,8},{8,0},{16,24},{24,16},{32,40},{40,32},{48,56},{56,48},{64,72... | collective-permute-start | bytes 835592 | tf_op jit(solution)/shard_map/ppermute | solution.py:156
  32.9 26.2 %all-to-all-start.1 = ((f32[8,32,512]{2,1,0:T(8,128)}), f32[8,32,512]{2,1,0:T(8,128)S(1)}, u32[]{:S(2)}, u32[]{:S(2)}) async-start(f32[8,32,512]{2,1,0:T(8,128)} %place.1), calls=%async_computation.1 | async-start | bytes 1048576 | tf_op jit(solution)/shard_map/all_to_all | solution.py:166
  41.1 7.3 %collective-permute-start = (f32[4,32,512]{2,1,0:T(8,128)S(1)}, f32[4,32,512]{2,1,0:T(8,128)S(1)}, u32[]{:S(2)}, u32[]{:S(2)}) collective-permute-start(f32[4,32,512]{2,1,0:T(8,128)S(1)} %slice_bitcast_fusion), channel_id=1, source_target_pairs={{0,1},{1,0},{2,3},{3,2},{4,5},{5,4},{6,7},{7,6},{8,9},{9,8},{10,11... | collective-permute-start | bytes 786440 | tf_op jit(solution)/shard_map/ppermute | solution.py:141
  48.5 10.6 %collective-permute-start.1 = (f32[32,512]{1,0:T(8,128)S(1)}, f32[32,512]{1,0:T(8,128)S(1)}, u32[]{:S(2)}, u32[]{:S(2)}) collective-permute-start(f32[32,512]{1,0:T(8,128)S(1)} %get-tuple-element.9), channel_id=1, source_target_pairs={{0,2},{1,3},{2,4},{3,5},{4,6},{5,7},{6,0},{7,1},{8,10},{9,11},{10,... | collective-permute-start | bytes 196616 | tf_op jit(solution)/shard_map/ppermute | solution.py:169
  48.6 10.5 %collective-permute-start.3 = (f32[32,512]{1,0:T(8,128)S(1)}, f32[32,512]{1,0:T(8,128)S(1)}, u32[]{:S(2)}, u32[]{:S(2)}) collective-permute-start(f32[32,512]{1,0:T(8,128)S(1)} %get-tuple-element.10), channel_id=1, source_target_pairs={{0,6},{1,7},{2,0},{3,1},{4,2},{5,3},{6,4},{7,5},{8,14},{9,15},{10,... | collective-permute-start | bytes 196616 | tf_op jit(solution)/shard_map/ppermute | solution.py:169
  51.2 7.9 %collective-permute-start.2 = (f32[32,512]{1,0:T(8,128)S(1)}, f32[32,512]{1,0:T(8,128)S(1)}, u32[]{:S(2)}, u32[]{:S(2)}) collective-permute-start(f32[32,512]{1,0:T(8,128)S(1)} %get-tuple-element.11), channel_id=1, source_target_pairs={{0,4},{1,5},{2,6},{3,7},{4,0},{5,1},{6,2},{7,3},{8,12},{9,13},{10,... | collective-permute-start | bytes 196616 | tf_op jit(solution)/shard_map/ppermute | solution.py:169

commit v3 on v2

v3 whole, which is shorter than its diff:
```python
import jax
import jax.numpy as jnp
from jax import lax
from jax.experimental import pallas as pl
from jax.experimental.pallas import tpu as pltpu
from jax.sharding import PartitionSpec as P

BLKS = 8
GRPS = 32
ZS = 8
YS = 4
Z_ORDER = (4, 3, 5, 2, 6, 1, 7)
Z_AFTER = {1: 2, 7: 6}
VMEM_BYTES = 32 * 1024 * 1024


def split(x):
    high = x.astype(jnp.bfloat16)
    low = (x - high.astype(jnp.float32)).astype(jnp.bfloat16)
    return high, low


def product(p, tile, contract):
    count = p.shape[0]
    p_parts = jnp.concatenate(split(p), axis=0)
    t_high, t_low = split(tile)
    dims = (((1,), (contract,)), ((), ()))
    first = lax.dot_general(p_parts, t_high, dims, preferred_element_type=jnp.float32)
    second = lax.dot_general(p_parts, t_low, dims, preferred_element_type=jnp.float32)
    both = first + second
    return both[:count] + both[count:]


def joined(ref):
    return jnp.concatenate([ref[:, q, :] for q in range(4)], axis=1)


def own_kernel(direction, out, own, sem):
    copy = pltpu.make_async_copy(direction.at[:, lax.axis_index("grp")], own, sem)
    copy.start()
    copy.wait()
    out[...] = joined(own)


def rows_kernel(pairs, direction, tiles, out, held, picked, sem):
    k_count = tiles.shape[0]
    picks, loads = [], []
    for k in range(k_count):
        group = pairs[1, k] // BLKS
        picks.append(pltpu.make_async_copy(direction.at[:, group], picked.at[k], sem.at[0, k]))
        loads.append(pltpu.make_async_copy(tiles.at[k], held.at[k], sem.at[1, k]))
        picks[k].start()
        loads[k].start()
    out[...] = jnp.zeros_like(out)
    for k in range(k_count):
        picks[k].wait()
        loads[k].wait()
        out[pairs[0, k] % BLKS] += product(joined(picked.at[k]), held[k], 1)


def mirror_kernel(pairs, *refs):
    *got, tiles, out, held = refs
    k_count = tiles.shape[0]
    cols = got[0].shape[0]
    b = pairs[1, 0] % BLKS
    for k in range(k_count):
        i, j = pairs[0, k], pairs[1, k]
        r = i % BLKS
        source = (b // 2 + YS - r // 2) % YS * 2 + (r + b) % 2
        for at, block in enumerate(got):

            @pl.when(source == at)
            def _():
                held[k] = block[...]

        out[pl.ds(k * cols, cols)] = product(held[k], tiles[k], 0)
        place = jnp.where(i != j, j // BLKS, -1).astype(jnp.float32)
        out[k_count * cols:, pl.ds(k * 128, 128)] = jnp.full((8, 128), place, jnp.float32)


def group_of(part, k, k_count, cols):
    return part[pl.ds(k_count * cols, 1), pl.ds(k * 128, 128)][0, 0].astype(jnp.int32)


def add_parts(grp, groups, parts, out):
    cols = out.shape[1]
    k_count = len(groups) // len(parts)
    for at, m in enumerate(groups):

        @pl.when((m >= 0) & (m % 4 == grp % 4))
        def _():
            out[(m // 4 + ZS - grp // 4) % ZS] += parts[at // k_count][pl.ds(at % k_count * cols, cols)]


def place_kernel(pairs, own, other, out):
    cols, width = out.shape[1:]
    k_count = width // 128
    groups = [jnp.where(pairs[0, k] != pairs[1, k], pairs[1, k] // BLKS, -1) for k in range(k_count)]
    groups += [group_of(other, k, k_count, cols) for k in range(k_count)]
    out[...] = jnp.zeros_like(out)
    add_parts(pairs[0, 0] // BLKS, groups, [own, other], out)


def join_kernel(pairs, base, one, two, *refs):
    *outs, total = refs
    cols, width = total.shape[1:]
    k_count = width // 128
    groups = [group_of(part, k, k_count, cols) for part in (one, two) for k in range(k_count)]
    total[...] = base[...]
    add_parts(pairs[0, 0] // BLKS, groups, [one, two], total)
    for at, out in enumerate(outs):
        out[...] = total[at]


def shards(tiles, pairs, direction):
    k_count, width, _ = tiles.shape
    cols = direction.shape[0]
    f32 = jnp.float32
    block = jax.ShapeDtypeStruct((cols, width), f32)
    smem = pl.BlockSpec(memory_space=pltpu.SMEM)
    vmem = pl.BlockSpec(memory_space=pltpu.VMEM)
    hbm = pl.BlockSpec(memory_space=pltpu.HBM)
    params = pltpu.CompilerParams(vmem_limit_bytes=VMEM_BYTES)
    x_swap = [(b, b ^ 1) for b in range(BLKS)]
    pairs = pairs.T
    lanes = pltpu.with_memory_space_constraint(direction.reshape(cols, GRPS, 4, 128), pltpu.HBM)

    own = pl.pallas_call(
        own_kernel,
        out_shape=block,
        in_specs=[hbm],
        out_specs=vmem,
        scratch_shapes=[pltpu.VMEM((cols, 4, 128), f32), pltpu.SemaphoreType.DMA],
        compiler_params=params,
        name="own",
    )(lanes)
    near_own = lax.ppermute(own, "blk", x_swap)
    got = [own, near_own]
    for step in range(1, YS):
        swap = [(b, (b + 2 * step) % BLKS) for b in range(BLKS)]
        got += [lax.ppermute(own, "blk", swap), lax.ppermute(near_own, "blk", swap)]

    rows, held = pl.pallas_call(
        rows_kernel,
        out_shape=[jax.ShapeDtypeStruct((BLKS, cols, width), f32), jax.ShapeDtypeStruct(tiles.shape, f32)],
        in_specs=[smem, hbm, hbm],
        out_specs=[vmem, vmem],
        scratch_shapes=[pltpu.VMEM((k_count, cols, 4, 128), f32), pltpu.SemaphoreType.DMA((2, k_count))],
        compiler_params=params,
        cost_estimate=pl.CostEstimate(flops=600_000_000, bytes_accessed=10_000_000, transcendentals=0),
        name="rows",
    )(pairs, lanes, pltpu.with_memory_space_constraint(tiles, pltpu.HBM))

    terms = pl.pallas_call(
        mirror_kernel,
        out_shape=jax.ShapeDtypeStruct((k_count * cols + 8, width), f32),
        in_specs=[smem] + [vmem] * (BLKS + 1),
        out_specs=vmem,
        scratch_shapes=[pltpu.VMEM((k_count, cols, width), f32)],
        compiler_params=params,
        name="mirror",
    )(pairs, *got, held)
    over_x = lax.ppermute(terms, "grp", [(g, g ^ 2) for g in range(GRPS)])
    over_core = lax.ppermute(terms, "grp", [(g, g ^ 1) for g in range(GRPS)])
    over_both = lax.ppermute(over_x, "grp", [(g, g ^ 1) for g in range(GRPS)])
    rows = lax.all_to_all(rows, "blk", 0, 0, tiled=True)
    part = pl.pallas_call(
        place_kernel,
        out_shape=jax.ShapeDtypeStruct((ZS, cols, width), f32),
        in_specs=[smem, vmem, vmem],
        out_specs=vmem,
        compiler_params=params,
        name="place",
    )(pairs, terms, over_core)
    parts = pl.pallas_call(
        join_kernel,
        out_shape=[block] * ZS,
        in_specs=[smem, vmem, vmem, vmem],
        out_specs=[vmem] * ZS,
        scratch_shapes=[pltpu.VMEM((ZS, cols, width), f32)],
        compiler_params=params,
        name="join",
    )(pairs, part, over_x, over_both)
    parts = list(parts)
    for step in Z_ORDER:
        if step in Z_AFTER:
            parts[step], parts[Z_AFTER[step]] = lax.optimization_barrier((parts[step], parts[Z_AFTER[step]]))
        parts[step] = lax.ppermute(parts[step], "grp", [(g, (g + 4 * step) % GRPS) for g in range(GRPS)])
    total = jnp.sum(rows, axis=0)
    for part in parts:
        total = total + part
    return total.reshape(cols, 1, 1, width)


def solution(mesh):
    placed = (P(("grp", "blk"), None, None), P(("grp", "blk"), None), P(None, None, "blk", None))
    return jax.shard_map(
        shards, mesh=mesh, in_specs=placed, out_specs=P(None, "grp", "blk", None), check_vma=False
    )
```

time: 60.1 us -> 54.6 us (0.908)
  the two profiles are of different devices: /device:TPU:1 before, /device:TPU:60 now
where the time goes in v3:
time: 54.6 us; the launch traced here: 54.3 us
  starting transfers between devices  33.6 us (62%)
  waiting for transfers between devices  10.3 us (19%)
  Pallas kernels  8.84 us (16%)
  local copies, waits for them, and re-layouts  1.38 us (3%)
    ppermute x7, starting transfers between devices, shards(): lax.ppermute(parts[step], 'grp', [(g, (g + 4 * step) % GRPS) for g in ran...  17.6 us
    ppermute x6, starting transfers between devices, shards(): got += [lax.ppermute(own, 'blk', swap), lax.ppermute(near_own, 'blk', swap)]  8.79 us
    ppermute x7, waiting for transfers between devices, shards(): lax.ppermute(parts[step], 'grp', [(g, (g + 4 * step) % GRPS) for g in ran...  5.4 us
    all_to_all x1, starting transfers between devices, shards(): rows = lax.all_to_all(rows, 'blk', 0, 0, tiled=True)  5.1 us
    pallas_call x1, Pallas kernels, shards(): pl.pallas_call(rows_kernel, out_shape=[jax.ShapeDtypeStruct((BLKS, cols,...  4.52 us
    ppermute x1, waiting for transfers between devices, shards(): over_x = lax.ppermute(terms, 'grp', [(g, g ^ 2) for g in range(GRPS)])  4.03 us
    pallas_call x1, Pallas kernels, shards(): pl.pallas_call(mirror_kernel, out_shape=jax.ShapeDtypeStruct((k_count * c...  1.99 us
    ppermute x1, starting transfers between devices, shards(): near_own = lax.ppermute(own, 'blk', x_swap)  1.28 us
  transfers between devices with their start and end apart: 18, of which 4 were waited for; matrix products, arithmetic and copies ran while one was open for 0% of the time, Pallas kernels for 11%

profile of v3, /device:TPU:60, one launch (start us, length us, event | category | flops | bytes accessed | tf_op | source)
XLA Modules:
  0.0 54.3 jit_solution(2773077336675421740)
XLA Ops:
  0.0 0.9 %own.1.refs_0_ = f32[32,512]{1,0:T(8,128)S(1)} custom-call(f32[32,32,4,128]{3,2,1,0:T(4,128)} %bitcast.8), custom_call_target="tpu_custom_call" | custom-call | tf_op jit(solution)/shard_map/own/pallas_call | solution.py:128
  0.9 1.3 %collective-permute-start = (f32[32,512]{1,0:T(8,128)S(1)}, f32[32,512]{1,0:T(8,128)S(1)}, u32[]{:S(2)}, u32[]{:S(2)}) collective-permute-start(f32[32,512]{1,0:T(8,128)S(1)} %own.1.refs_0_), channel_id=1, source_target_pairs={{0,1},{1,0},{2,3},{3,2},{4,5},{5,4},{6,7},{7,6},{8,9},{9,8},{10,11... | collective-permute-start | bytes 196616 | tf_op jit(solution)/shard_map/ppermute | solution.py:137
  2.2 0.7 %collective-permute-start.5 = (f32[32,512]{1,0:T(8,128)S(1)}, f32[32,512]{1,0:T(8,128)S(1)}, u32[]{:S(2)}, u32[]{:S(2)}) collective-permute-start(f32[32,512]{1,0:T(8,128)S(1)} %own.1.refs_0_), channel_id=1, source_target_pairs={{0,6},{1,7},{2,0},{3,1},{4,2},{5,3},{6,4},{7,5},{8,14},{9,15},{10,... | collective-permute-start | bytes 196616 | tf_op jit(solution)/shard_map/ppermute | solution.py:141
  2.9 0.9 %collective-permute-start.3 = (f32[32,512]{1,0:T(8,128)S(1)}, f32[32,512]{1,0:T(8,128)S(1)}, u32[]{:S(2)}, u32[]{:S(2)}) collective-permute-start(f32[32,512]{1,0:T(8,128)S(1)} %own.1.refs_0_), channel_id=1, source_target_pairs={{0,4},{1,5},{2,6},{3,7},{4,0},{5,1},{6,2},{7,3},{8,12},{9,13},{10,... | collective-permute-start | bytes 196616 | tf_op jit(solution)/shard_map/ppermute | solution.py:141
  3.9 2.2 %collective-permute-start.1 = (f32[32,512]{1,0:T(8,128)S(1)}, f32[32,512]{1,0:T(8,128)S(1)}, u32[]{:S(2)}, u32[]{:S(2)}) collective-permute-start(f32[32,512]{1,0:T(8,128)S(1)} %own.1.refs_0_), channel_id=1, source_target_pairs={{0,2},{1,3},{2,4},{3,5},{4,6},{5,7},{6,0},{7,1},{8,10},{9,11},{10,... | collective-permute-start | bytes 196616 | tf_op jit(solution)/shard_map/ppermute | solution.py:141
  6.3 2.2 %collective-permute-start.4 = (f32[32,512]{1,0:T(8,128)S(1)}, f32[32,512]{1,0:T(8,128)S(1)}, u32[]{:S(2)}, u32[]{:S(2)}) collective-permute-start(f32[32,512]{1,0:T(8,128)S(1)} %collective-permute-done.refs_1_), channel_id=1, source_target_pairs={{0,4},{1,5},{2,6},{3,7},{4,0},{5,1},{6,2},{7,3},{8,12},{9,13},{10,... | collective-permute-start | bytes 196616 | tf_op jit(solution)/shard_map/ppermute | solution.py:141
  8.5 2.5 %collective-permute-start.2 = (f32[32,512]{1,0:T(8,128)S(1)}, f32[32,512]{1,0:T(8,128)S(1)}, u32[]{:S(2)}, u32[]{:S(2)}) collective-permute-start(f32[32,512]{1,0:T(8,128)S(1)} %collective-permute-done.refs_1_), channel_id=1, source_target_pairs={{0,2},{1,3},{2,4},{3,5},{4,6},{5,7},{6,0},{7,1},{8,10},{9,11},{10,... | collective-permute-start | bytes 196616 | tf_op jit(solution)/shard_map/ppermute | solution.py:141
  11.7 4.5 %rows.1 = (f32[8,32,512]{2,1,0:T(8,128)}, f32[4,512,512]{2,1,0:T(8,128)S(1)}) custom-call(s32[2,4]{1,0:T(2,128)S(1)} %bitcast.4, f32[32,32,4,128]{3,2,1,0:T(4,128)} %bitcast.9, f32[4,512,512]{2,1,0:T(8,128)} %tiles.1), custom_call_target="tpu_custom_call" | custom-call | flops 600000000 | bytes 10000000 | tf_op jit(solution)/shard_map/rows/pallas_call | solution.py:143
  16.2 2.0 %mirror.1.own = f32[136,512]{1,0:T(8,128)S(1)} custom-call(s32[2,4]{1,0:T(2,128)S(1)} %bitcast.5, f32[32,512]{1,0:T(8,128)S(1)} %own.1.refs_0_, f32[32,512]{1,0:T(8,128)S(1)} %collective-permute-done.refs_1_, f32[32,512]{1,0:T(8,128)S(1)} %collective-permute-done.1.refs_2_, f32[32,512]{1,0:T(8,128)S(1)} %collective-permute-done.2.refs_3_, ...), custom_call_target="tpu_custom_call" | custom-call | tf_op jit(solution)/shard_map/mirror/pallas_call | solution.py:154
  18.2 0.9 %collective-permute-start.8 = (f32[136,512]{1,0:T(8,128)S(1)}, f32[136,512]{1,0:T(8,128)S(1)}, u32[]{:S(2)}, u32[]{:S(2)}) collective-permute-start(f32[136,512]{1,0:T(8,128)S(1)} %mirror.1.own), channel_id=1, source_target_pairs={{0,16},{8,24},{16,0},{24,8},{32,48},{40,56},{48,32},{56,40},{64,80... | collective-permute-start | bytes 835592 | tf_op jit(solution)/shard_map/ppermute | solution.py:163
  19.1 5.1 %all-to-all-start = ((f32[8,32,512]{2,1,0:T(8,128)}), f32[8,32,512]{2,1,0:T(8,128)S(1)}, u32[]{:S(2)}, u32[]{:S(2)}) async-start(f32[8,32,512]{2,1,0:T(8,128)} %get-tuple-element.19), calls=%async_computation | async-start | bytes 1048576 | tf_op jit(solution)/shard_map/all_to_all | solution.py:166
  24.2 4.0 %collective-permute-done.8.one = f32[136,512]{1,0:T(8,128)S(1)} collective-permute-done((f32[136,512]{1,0:T(8,128)S(1)}, f32[136,512]{1,0:T(8,128)S(1)}, u32[]{:S(2)}, u32[]{:S(2)}) %collective-permute-start.8) | collective-permute-done | bytes 278560 | tf_op jit(solution)/shard_map/ppermute | solution.py:163
  28.3 0.7 %place.1.base = f32[8,32,512]{2,1,0:T(8,128)S(1)} custom-call(s32[2,4]{1,0:T(2,128)S(1)} %bitcast.6, f32[136,512]{1,0:T(8,128)S(1)} %mirror.1.own, f32[136,512]{1,0:T(8,128)S(1)} %collective-permute-done.7.other), custom_call_target="tpu_custom_call" | custom-call | tf_op jit(solution)/shard_map/place/pallas_call | solution.py:167
  29.0 0.8 %collective-permute-done.9.two = f32[136,512]{1,0:T(8,128)S(1)} collective-permute-done((f32[136,512]{1,0:T(8,128)S(1)}, f32[136,512]{1,0:T(8,128)S(1)}, u32[]{:S(2)}, u32[]{:S(2)}) %collective-permute-start.9) | collective-permute-done | bytes 278560 | tf_op jit(solution)/shard_map/ppermute | solution.py:165
  29.8 0.7 %join.1 = (f32[32,512]{1,0:T(8,128)S(1)}, f32[32,512]{1,0:T(8,128)S(1)}, f32[32,512]{1,0:T(8,128)S(1)}, f32[32,512]{1,0:T(8,128)S(1)}, f32[32,512]{1,0:T(8,128)S...) custom-call(s32[2,4]{1,0:T(2,128)S(1)} %bitcast.7, f32[8,32,512]{2,1,0:T(8,128)S(1)} %place.1.base, ...), custom_call_target="tpu_custom_call" | custom-call | tf_op jit(solution)/shard_map/join/pallas_call | solution.py:175
  30.5 3.4 %collective-permute-start.10 = (f32[32,512]{1,0:T(8,128)S(1)}, f32[32,512]{1,0:T(8,128)S(1)}, u32[]{:S(2)}, u32[]{:S(2)}) collective-permute-start(f32[32,512]{1,0:T(8,128)S(1)} %get-tuple-element.23), channel_id=1, source_target_pairs={{0,64},{8,72},{16,80},{24,88},{32,96},{40,104},{48,112},{56,120},{... | collective-permute-start | bytes 196616 | tf_op jit(solution)/shard_map/ppermute | solution.py:188
  33.9 2.2 %collective-permute-start.15 = (f32[32,512]{1,0:T(8,128)S(1)}, f32[32,512]{1,0:T(8,128)S(1)}, u32[]{:S(2)}, u32[]{:S(2)}) collective-permute-start(f32[32,512]{1,0:T(8,128)S(1)} %get-tuple-element.30), channel_id=1, source_target_pairs={{0,192},{8,200},{16,208},{24,216},{32,224},{40,232},{48,240},{56,2... | collective-permute-start | bytes 196616 | tf_op jit(solution)/shard_map/ppermute | solution.py:188
  36.1 4.5 %collective-permute-start.12 = (f32[32,512]{1,0:T(8,128)S(1)}, f32[32,512]{1,0:T(8,128)S(1)}, u32[]{:S(2)}, u32[]{:S(2)}) collective-permute-start(f32[32,512]{1,0:T(8,128)S(1)} %get-tuple-element.26), channel_id=1, source_target_pairs={{0,96},{8,104},{16,112},{24,120},{32,128},{40,136},{48,144},{56,15... | collective-permute-start | bytes 196616 | tf_op jit(solution)/shard_map/ppermute | solution.py:188
  40.6 1.0 %collective-permute-start.13 = (f32[32,512]{1,0:T(8,128)S(1)}, f32[32,512]{1,0:T(8,128)S(1)}, u32[]{:S(2)}, u32[]{:S(2)}) collective-permute-start(f32[32,512]{1,0:T(8,128)S(1)} %get-tuple-element.27), channel_id=1, source_target_pairs={{0,128},{8,136},{16,144},{24,152},{32,160},{40,168},{48,176},{56,1... | collective-permute-start | bytes 196616 | tf_op jit(solution)/shard_map/ppermute | solution.py:188
  41.6 4.5 %collective-permute-start.14 = (f32[32,512]{1,0:T(8,128)S(1)}, f32[32,512]{1,0:T(8,128)S(1)}, u32[]{:S(2)}, u32[]{:S(2)}) collective-permute-start(f32[32,512]{1,0:T(8,128)S(1)} %get-tuple-element.28), channel_id=1, source_target_pairs={{0,160},{8,168},{16,176},{24,184},{32,192},{40,200},{48,208},{56,2... | collective-permute-start | bytes 196616 | tf_op jit(solution)/shard_map/ppermute | solution.py:188
  46.1 2.0 %collective-permute-start.16 = (f32[32,512]{1,0:T(8,128)S(1)}, f32[32,512]{1,0:T(8,128)S(1)}, u32[]{:S(2)}, u32[]{:S(2)}) collective-permute-start(f32[32,512]{1,0:T(8,128)S(1)} %get-tuple-element.32), channel_id=1, source_target_pairs={{0,224},{8,232},{16,240},{24,248},{32,0},{40,8},{48,16},{56,24},{6... | collective-permute-start | bytes 196616 | tf_op jit(solution)/shard_map/ppermute | solution.py:188
  48.2 4.3 %collective-permute-done.13 = f32[32,512]{1,0:T(8,128)S(1)} collective-permute-done((f32[32,512]{1,0:T(8,128)S(1)}, f32[32,512]{1,0:T(8,128)S(1)}, u32[]{:S(2)}, u32[]{:S(2)}) %collective-permute-start.13) | collective-permute-done | bytes 65568 | tf_op jit(solution)/shard_map/ppermute | solution.py:188
  52.5 1.1 %collective-permute-done.14 = f32[32,512]{1,0:T(8,128)S(1)} collective-permute-done((f32[32,512]{1,0:T(8,128)S(1)}, f32[32,512]{1,0:T(8,128)S(1)}, u32[]{:S(2)}, u32[]{:S(2)}) %collective-permute-start.14) | collective-permute-done | bytes 65568 | tf_op jit(solution)/shard_map/ppermute | solution.py:188
  53.6 0.7 %copy.4 = f32[32,1,1,512]{3,2,1,0:T(1,128)} copy(f32[32,1,1,512]{3,0,2,1:T(8,128)S(1)} %add_bitcast_fusion) | data formatting | bytes 131072 | tf_op jit(solution)/shard_map/reshape | solution.py:192
  (24 shorter events, 1.0 us)
Async XLA Ops:
  0.9 5.2 %collective-permute-start = (f32[32,512]{1,0:T(8,128)S(1)}, f32[32,512]{1,0:T(8,128)S(1)}, u32[]{:S(2)}, u32[]{:S(2)}) collective-permute-start(f32[32,512]{1,0:T(8,128)S(1)} %own.1.refs_0_), channel_id=1, source_target_pairs={{0,1},{1,0},{2,3},{3,2},{4,5},{5,4},{6,7},{7,6},{8,9},{9,8},{10,11... | collective-permute-start | bytes 196616 | tf_op jit(solution)/shard_map/ppermute | solution.py:137
  2.2 6.3 %collective-permute-start.5 = (f32[32,512]{1,0:T(8,128)S(1)}, f32[32,512]{1,0:T(8,128)S(1)}, u32[]{:S(2)}, u32[]{:S(2)}) collective-permute-start(f32[32,512]{1,0:T(8,128)S(1)} %own.1.refs_0_), channel_id=1, source_target_pairs={{0,6},{1,7},{2,0},{3,1},{4,2},{5,3},{6,4},{7,5},{8,14},{9,15},{10,... | collective-permute-start | bytes 196616 | tf_op jit(solution)/shard_map/ppermute | solution.py:141
  2.9 13.3 %collective-permute-start.3 = (f32[32,512]{1,0:T(8,128)S(1)}, f32[32,512]{1,0:T(8,128)S(1)}, u32[]{:S(2)}, u32[]{:S(2)}) collective-permute-start(f32[32,512]{1,0:T(8,128)S(1)} %own.1.refs_0_), channel_id=1, source_target_pairs={{0,4},{1,5},{2,6},{3,7},{4,0},{5,1},{6,2},{7,3},{8,12},{9,13},{10,... | collective-permute-start | bytes 196616 | tf_op jit(solution)/shard_map/ppermute | solution.py:141
  3.9 12.3 %collective-permute-start.1 = (f32[32,512]{1,0:T(8,128)S(1)}, f32[32,512]{1,0:T(8,128)S(1)}, u32[]{:S(2)}, u32[]{:S(2)}) collective-permute-start(f32[32,512]{1,0:T(8,128)S(1)} %own.1.refs_0_), channel_id=1, source_target_pairs={{0,2},{1,3},{2,4},{3,5},{4,6},{5,7},{6,0},{7,1},{8,10},{9,11},{10,... | collective-permute-start | bytes 196616 | tf_op jit(solution)/shard_map/ppermute | solution.py:141
  6.0 10.2 %collective-permute-start.6 = (f32[32,512]{1,0:T(8,128)S(1)}, f32[32,512]{1,0:T(8,128)S(1)}, u32[]{:S(2)}, u32[]{:S(2)}) collective-permute-start(f32[32,512]{1,0:T(8,128)S(1)} %collective-permute-done.refs_1_), channel_id=1, source_target_pairs={{0,6},{1,7},{2,0},{3,1},{4,2},{5,3},{6,4},{7,5},{8,14},{9,15},{10,... | collective-permute-start | bytes 196616 | tf_op jit(solution)/shard_map/ppermute | solution.py:141
  6.3 9.9 %collective-permute-start.4 = (f32[32,512]{1,0:T(8,128)S(1)}, f32[32,512]{1,0:T(8,128)S(1)}, u32[]{:S(2)}, u32[]{:S(2)}) collective-permute-start(f32[32,512]{1,0:T(8,128)S(1)} %collective-permute-done.refs_1_), channel_id=1, source_target_pairs={{0,4},{1,5},{2,6},{3,7},{4,0},{5,1},{6,2},{7,3},{8,12},{9,13},{10,... | collective-permute-start | bytes 196616 | tf_op jit(solution)/shard_map/ppermute | solution.py:141
  8.5 7.8 %collective-permute-start.2 = (f32[32,512]{1,0:T(8,128)S(1)}, f32[32,512]{1,0:T(8,128)S(1)}, u32[]{:S(2)}, u32[]{:S(2)}) collective-permute-start(f32[32,512]{1,0:T(8,128)S(1)} %collective-permute-done.refs_1_), channel_id=1, source_target_pairs={{0,2},{1,3},{2,4},{3,5},{4,6},{5,7},{6,0},{7,1},{8,10},{9,11},{10,... | collective-permute-start | bytes 196616 | tf_op jit(solution)/shard_map/ppermute | solution.py:141
  11.0 0.7 %copy-start = (s32[4,2]{0,1:T(2,128)S(1)}, s32[4,2]{0,1:T(2,128)}, u32[]{:S(2)}) copy-start(s32[4,2]{0,1:T(2,128)} %param.4) | copy-start | bytes 100
  16.2 12.1 %copy-start.1 = (s32[4,2]{0,1:T(2,128)S(1)}, s32[4,2]{0,1:T(2,128)}, u32[]{:S(2)}) copy-start(s32[4,2]{0,1:T(2,128)} %param.4) | copy-start | bytes 100
  18.2 10.0 %collective-permute-start.8 = (f32[136,512]{1,0:T(8,128)S(1)}, f32[136,512]{1,0:T(8,128)S(1)}, u32[]{:S(2)}, u32[]{:S(2)}) collective-permute-start(f32[136,512]{1,0:T(8,128)S(1)} %mirror.1.own), channel_id=1, source_target_pairs={{0,16},{8,24},{16,0},{24,8},{32,48},{40,56},{48,32},{56,40},{64,80... | collective-permute-start | bytes 835592 | tf_op jit(solution)/shard_map/ppermute | solution.py:163
  19.1 29.0 %all-to-all-start = ((f32[8,32,512]{2,1,0:T(8,128)}), f32[8,32,512]{2,1,0:T(8,128)S(1)}, u32[]{:S(2)}, u32[]{:S(2)}) async-start(f32[8,32,512]{2,1,0:T(8,128)} %get-tuple-element.19), calls=%async_computation | async-start | bytes 1048576 | tf_op jit(solution)/shard_map/all_to_all | solution.py:166
  24.2 4.0 %collective-permute-start.7 = (f32[136,512]{1,0:T(8,128)S(1)}, f32[136,512]{1,0:T(8,128)S(1)}, u32[]{:S(2)}, u32[]{:S(2)}) collective-permute-start(f32[136,512]{1,0:T(8,128)S(1)} %mirror.1.own), channel_id=1, source_target_pairs={{0,8},{8,0},{16,24},{24,16},{32,40},{40,32},{48,56},{56,48},{64,72... | collective-permute-start | bytes 835592 | tf_op jit(solution)/shard_map/ppermute | solution.py:164
  28.3 1.6 %collective-permute-start.9 = (f32[136,512]{1,0:T(8,128)S(1)}, f32[136,512]{1,0:T(8,128)S(1)}, u32[]{:S(2)}, u32[]{:S(2)}) collective-permute-start(f32[136,512]{1,0:T(8,128)S(1)} %collective-permute-done.8.one), channel_id=1, source_target_pairs={{0,8},{8,0},{16,24},{24,16},{32,40},{40,32},{48,56},{56,48},{64,72... | collective-permute-start | bytes 835592 | tf_op jit(solution)/shard_map/ppermute | solution.py:165
  30.5 15.5 %collective-permute-start.10 = (f32[32,512]{1,0:T(8,128)S(1)}, f32[32,512]{1,0:T(8,128)S(1)}, u32[]{:S(2)}, u32[]{:S(2)}) collective-permute-start(f32[32,512]{1,0:T(8,128)S(1)} %get-tuple-element.23), channel_id=1, source_target_pairs={{0,64},{8,72},{16,80},{24,88},{32,96},{40,104},{48,112},{56,120},{... | collective-permute-start | bytes 196616 | tf_op jit(solution)/shard_map/ppermute | solution.py:188
  33.9 12.2 %collective-permute-start.15 = (f32[32,512]{1,0:T(8,128)S(1)}, f32[32,512]{1,0:T(8,128)S(1)}, u32[]{:S(2)}, u32[]{:S(2)}) collective-permute-start(f32[32,512]{1,0:T(8,128)S(1)} %get-tuple-element.30), channel_id=1, source_target_pairs={{0,192},{8,200},{16,208},{24,216},{32,224},{40,232},{48,240},{56,2... | collective-permute-start | bytes 196616 | tf_op jit(solution)/shard_map/ppermute | solution.py:188
  36.1 12.1 %collective-permute-start.12 = (f32[32,512]{1,0:T(8,128)S(1)}, f32[32,512]{1,0:T(8,128)S(1)}, u32[]{:S(2)}, u32[]{:S(2)}) collective-permute-start(f32[32,512]{1,0:T(8,128)S(1)} %get-tuple-element.26), channel_id=1, source_target_pairs={{0,96},{8,104},{16,112},{24,120},{32,128},{40,136},{48,144},{56,15... | collective-permute-start | bytes 196616 | tf_op jit(solution)/shard_map/ppermute | solution.py:188
  40.6 11.8 %collective-permute-start.13 = (f32[32,512]{1,0:T(8,128)S(1)}, f32[32,512]{1,0:T(8,128)S(1)}, u32[]{:S(2)}, u32[]{:S(2)}) collective-permute-start(f32[32,512]{1,0:T(8,128)S(1)} %get-tuple-element.27), channel_id=1, source_target_pairs={{0,128},{8,136},{16,144},{24,152},{32,160},{40,168},{48,176},{56,1... | collective-permute-start | bytes 196616 | tf_op jit(solution)/shard_map/ppermute | solution.py:188
  41.6 11.9 %collective-permute-start.14 = (f32[32,512]{1,0:T(8,128)S(1)}, f32[32,512]{1,0:T(8,128)S(1)}, u32[]{:S(2)}, u32[]{:S(2)}) collective-permute-start(f32[32,512]{1,0:T(8,128)S(1)} %get-tuple-element.28), channel_id=1, source_target_pairs={{0,160},{8,168},{16,176},{24,184},{32,192},{40,200},{48,208},{56,2... | collective-permute-start | bytes 196616 | tf_op jit(solution)/shard_map/ppermute | solution.py:188
  46.1 7.5 %collective-permute-start.11 = (f32[32,512]{1,0:T(8,128)S(1)}, f32[32,512]{1,0:T(8,128)S(1)}, u32[]{:S(2)}, u32[]{:S(2)}) collective-permute-start(f32[32,512]{1,0:T(8,128)S(1)} %get-tuple-element.24), channel_id=1, source_target_pairs={{0,32},{8,40},{16,48},{24,56},{32,64},{40,72},{48,80},{56,88},{64,... | collective-permute-start | bytes 196616 | tf_op jit(solution)/shard_map/ppermute | solution.py:188
  46.1 7.5 %collective-permute-start.16 = (f32[32,512]{1,0:T(8,128)S(1)}, f32[32,512]{1,0:T(8,128)S(1)}, u32[]{:S(2)}, u32[]{:S(2)}) collective-permute-start(f32[32,512]{1,0:T(8,128)S(1)} %get-tuple-element.32), channel_id=1, source_target_pairs={{0,224},{8,232},{16,240},{24,248},{32,0},{40,8},{48,16},{56,24},{6... | collective-permute-start | bytes 196616 | tf_op jit(solution)/shard_map/ppermute | solution.py:188

commit v4 on v3

--- a/solution.py
+++ b/solution.py
@@ -11,6 +11,7 @@
 YS = 4
 Z_ORDER = (4, 3, 5, 2, 6, 1, 7)
 Z_AFTER = {1: 2, 7: 6}
+X_AFTER = 6
 VMEM_BYTES = 32 * 1024 * 1024
 
 
@@ -55,7 +56,8 @@
     for k in range(k_count):
         picks[k].wait()
         loads[k].wait()
-        out[pairs[0, k] % BLKS] += product(joined(picked.at[k]), held[k], 1)
+        r, b = pairs[0, k] % BLKS, pairs[1, k] % BLKS
+        out[r // 2, (r + b) % 2] += product(joined(picked.at[k]), held[k], 1)
 
 
 def mirror_kernel(pairs, *refs):
@@ -142,7 +144,7 @@
 
     rows, held = pl.pallas_call(
         rows_kernel,
-        out_shape=[jax.ShapeDtypeStruct((BLKS, cols, width), f32), jax.ShapeDtypeStruct(tiles.shape, f32)],
+        out_shape=[jax.ShapeDtypeStruct((YS, 2, cols, width), f32), jax.ShapeDtypeStruct(tiles.shape, f32)],
         in_specs=[smem, hbm, hbm],
         out_specs=[vmem, vmem],
         scratch_shapes=[pltpu.VMEM((k_count, cols, 4, 128), f32), pltpu.SemaphoreType.DMA((2, k_count))],
@@ -163,7 +165,8 @@
     over_x = lax.ppermute(terms, "grp", [(g, g ^ 2) for g in range(GRPS)])
     over_core = lax.ppermute(terms, "grp", [(g, g ^ 1) for g in range(GRPS)])
     over_both = lax.ppermute(over_x, "grp", [(g, g ^ 1) for g in range(GRPS)])
-    rows = lax.all_to_all(rows, "blk", 0, 0, tiled=True)
+    along_y = [[2 * y + x for y in range(YS)] for x in range(2)]
+    rows = lax.all_to_all(rows, "blk", 0, 0, tiled=True, axis_index_groups=along_y)
     part = pl.pallas_call(
         place_kernel,
         out_shape=jax.ShapeDtypeStruct((ZS, cols, width), f32),
@@ -186,7 +189,9 @@
         if step in Z_AFTER:
             parts[step], parts[Z_AFTER[step]] = lax.optimization_barrier((parts[step], parts[Z_AFTER[step]]))
         parts[step] = lax.ppermute(parts[step], "grp", [(g, (g + 4 * step) % GRPS) for g in range(GRPS)])
-    total = jnp.sum(rows, axis=0)
+    rows, parts[X_AFTER] = lax.optimization_barrier((rows, parts[X_AFTER]))
+    row_sum = jnp.sum(rows, axis=0)
+    total = row_sum[0] + lax.ppermute(row_sum[1], "blk", x_swap)
     for part in parts:
         total = total + part
     return total.reshape(cols, 1, 1, width)

time: 54.6 us -> 53.7 us (0.984)
  the two profiles are of different devices: /device:TPU:60 before, /device:TPU:8 now
where the time goes in v4:
time: 53.7 us; the launch traced here: 53.5 us
  starting transfers between devices  36.6 us (68%)
  Pallas kernels  8.81 us (16%)
  waiting for transfers between devices  6.39 us (12%)
  local copies, waits for them, and re-layouts  1.39 us (3%)
    ppermute x7, starting transfers between devices, shards(): lax.ppermute(parts[step], 'grp', [(g, (g + 4 * step) % GRPS) for g in ran...  18.3 us
    ppermute x6, starting transfers between devices, shards(): got += [lax.ppermute(own, 'blk', swap), lax.ppermute(near_own, 'blk', swap)]  8.79 us
    ppermute x7, waiting for transfers between devices, shards(): lax.ppermute(parts[step], 'grp', [(g, (g + 4 * step) % GRPS) for g in ran...  4.82 us
    all_to_all x1, starting transfers between devices, shards(): lax.all_to_all(rows, 'blk', 0, 0, tiled=True, axis_index_groups=along_y)  4.72 us
    pallas_call x1, Pallas kernels, shards(): pl.pallas_call(rows_kernel, out_shape=[jax.ShapeDtypeStruct((YS, 2, cols,...  4.53 us
    ppermute x1, starting transfers between devices, shards(): over_x = lax.ppermute(terms, 'grp', [(g, g ^ 2) for g in range(GRPS)])  2.81 us
    pallas_call x1, Pallas kernels, shards(): pl.pallas_call(mirror_kernel, out_shape=jax.ShapeDtypeStruct((k_count * c...  1.99 us
    ppermute x1, starting transfers between devices, shards(): near_own = lax.ppermute(own, 'blk', x_swap)  1.58 us
  transfers between devices with their start and end apart: 19, of which 6 were waited for; matrix products, arithmetic and copies ran while one was open for 0% of the time, Pallas kernels for 11%

profile of v4, /device:TPU:8, one launch (start us, length us, event | category | flops | bytes accessed | tf_op | source)
XLA Modules:
  0.0 53.5 jit_solution(16027471187459728492)
XLA Ops:
  0.0 0.9 %own.1.refs_0_ = f32[32,512]{1,0:T(8,128)S(1)} custom-call(f32[32,32,4,128]{3,2,1,0:T(4,128)} %bitcast.32), custom_call_target="tpu_custom_call" | custom-call | tf_op jit(solution)/shard_map/own/pallas_call | solution.py:130
  0.9 1.6 %collective-permute-start = (f32[32,512]{1,0:T(8,128)S(1)}, f32[32,512]{1,0:T(8,128)S(1)}, u32[]{:S(2)}, u32[]{:S(2)}) collective-permute-start(f32[32,512]{1,0:T(8,128)S(1)} %own.1.refs_0_), channel_id=1, source_target_pairs={{0,1},{1,0},{2,3},{3,2},{4,5},{5,4},{6,7},{7,6},{8,9},{9,8},{10,11... | collective-permute-start | bytes 196616 | tf_op jit(solution)/shard_map/ppermute | solution.py:139
  2.5 0.8 %collective-permute-start.5 = (f32[32,512]{1,0:T(8,128)S(1)}, f32[32,512]{1,0:T(8,128)S(1)}, u32[]{:S(2)}, u32[]{:S(2)}) collective-permute-start(f32[32,512]{1,0:T(8,128)S(1)} %own.1.refs_0_), channel_id=1, source_target_pairs={{0,6},{1,7},{2,0},{3,1},{4,2},{5,3},{6,4},{7,5},{8,14},{9,15},{10,... | collective-permute-start | bytes 196616 | tf_op jit(solution)/shard_map/ppermute | solution.py:143
  3.3 2.3 %collective-permute-start.3 = (f32[32,512]{1,0:T(8,128)S(1)}, f32[32,512]{1,0:T(8,128)S(1)}, u32[]{:S(2)}, u32[]{:S(2)}) collective-permute-start(f32[32,512]{1,0:T(8,128)S(1)} %own.1.refs_0_), channel_id=1, source_target_pairs={{0,4},{1,5},{2,6},{3,7},{4,0},{5,1},{6,2},{7,3},{8,12},{9,13},{10,... | collective-permute-start | bytes 196616 | tf_op jit(solution)/shard_map/ppermute | solution.py:143
  5.5 1.9 %collective-permute-start.1 = (f32[32,512]{1,0:T(8,128)S(1)}, f32[32,512]{1,0:T(8,128)S(1)}, u32[]{:S(2)}, u32[]{:S(2)}) collective-permute-start(f32[32,512]{1,0:T(8,128)S(1)} %own.1.refs_0_), channel_id=1, source_target_pairs={{0,2},{1,3},{2,4},{3,5},{4,6},{5,7},{6,0},{7,1},{8,10},{9,11},{10,... | collective-permute-start | bytes 196616 | tf_op jit(solution)/shard_map/ppermute | solution.py:143
  7.5 1.3 %collective-permute-start.4 = (f32[32,512]{1,0:T(8,128)S(1)}, f32[32,512]{1,0:T(8,128)S(1)}, u32[]{:S(2)}, u32[]{:S(2)}) collective-permute-start(f32[32,512]{1,0:T(8,128)S(1)} %collective-permute-done.refs_1_), channel_id=1, source_target_pairs={{0,4},{1,5},{2,6},{3,7},{4,0},{5,1},{6,2},{7,3},{8,12},{9,13},{10,... | collective-permute-start | bytes 196616 | tf_op jit(solution)/shard_map/ppermute | solution.py:143
  8.9 2.4 %collective-permute-start.2 = (f32[32,512]{1,0:T(8,128)S(1)}, f32[32,512]{1,0:T(8,128)S(1)}, u32[]{:S(2)}, u32[]{:S(2)}) collective-permute-start(f32[32,512]{1,0:T(8,128)S(1)} %collective-permute-done.refs_1_), channel_id=1, source_target_pairs={{0,2},{1,3},{2,4},{3,5},{4,6},{5,7},{6,0},{7,1},{8,10},{9,11},{10,... | collective-permute-start | bytes 196616 | tf_op jit(solution)/shard_map/ppermute | solution.py:143
  11.3 0.7 %copy-done = s32[4,2]{0,1:T(2,128)S(1)} copy-done((s32[4,2]{0,1:T(2,128)S(1)}, s32[4,2]{0,1:T(2,128)}, u32[]{:S(2)}) %copy-start) | copy-done | bytes 56
  12.0 4.5 %rows.1 = (f32[4,2,32,512]{3,2,1,0:T(8,128)}, f32[4,512,512]{2,1,0:T(8,128)S(1)}) custom-call(s32[2,4]{1,0:T(2,128)S(1)} %bitcast.28, f32[32,32,4,128]{3,2,1,0:T(4,128)} %bitcast.33, f32[4,512,512]{2,1,0:T(8,128)} %tiles.1), custom_call_target="tpu_custom_call" | custom-call | flops 600000000 | bytes 10000000 | tf_op jit(solution)/shard_map/rows/pallas_call | solution.py:145
  16.6 2.0 %mirror.1.own = f32[136,512]{1,0:T(8,128)S(1)} custom-call(s32[2,4]{1,0:T(2,128)S(1)} %bitcast.29, f32[32,512]{1,0:T(8,128)S(1)} %own.1.refs_0_, f32[32,512]{1,0:T(8,128)S(1)} %collective-permute-done.refs_1_, f32[32,512]{1,0:T(8,128)S(1)} %collective-permute-done.1.refs_2_, f32[32,512]{1,0:T(8,128)S(1)} %collective-permute-done.2.refs_3_, ...), custom_call_target="tpu_custom_call" | custom-call | tf_op jit(solution)/shard_map/mirror/pallas_call | solution.py:156
  18.6 2.8 %collective-permute-start.8 = (f32[136,512]{1,0:T(8,128)S(1)}, f32[136,512]{1,0:T(8,128)S(1)}, u32[]{:S(2)}, u32[]{:S(2)}) collective-permute-start(f32[136,512]{1,0:T(8,128)S(1)} %mirror.1.own), channel_id=1, source_target_pairs={{0,16},{8,24},{16,0},{24,8},{32,48},{40,56},{48,32},{56,40},{64,80... | collective-permute-start | bytes 835592 | tf_op jit(solution)/shard_map/ppermute | solution.py:165
  21.4 4.7 %all-to-all-start = ((f32[4,2,32,512]{3,2,1,0:T(8,128)}), f32[4,2,32,512]{3,2,1,0:T(8,128)S(1)}, u32[]{:S(2)}, u32[]{:S(2)}) async-start(f32[4,2,32,512]{3,2,1,0:T(8,128)} %get-tuple-element.21), calls=%async_computation | async-start | bytes 1048576 | tf_op jit(solution)/shard_map/all_to_all | solution.py:169
  26.7 1.0 %collective-permute-done.7.other = f32[136,512]{1,0:T(8,128)S(1)} collective-permute-done((f32[136,512]{1,0:T(8,128)S(1)}, f32[136,512]{1,0:T(8,128)S(1)}, u32[]{:S(2)}, u32[]{:S(2)}) %collective-permute-start.7) | collective-permute-done | bytes 278560 | tf_op jit(solution)/shard_map/ppermute | solution.py:166
  27.6 0.7 %place.1.base = f32[8,32,512]{2,1,0:T(8,128)S(1)} custom-call(s32[2,4]{1,0:T(2,128)S(1)} %bitcast.30, f32[136,512]{1,0:T(8,128)S(1)} %mirror.1.own, f32[136,512]{1,0:T(8,128)S(1)} %collective-permute-done.7.other), custom_call_target="tpu_custom_call" | custom-call | tf_op jit(solution)/shard_map/place/pallas_call | solution.py:170
  28.4 0.7 %join.1 = (f32[32,512]{1,0:T(8,128)S(1)}, f32[32,512]{1,0:T(8,128)S(1)}, f32[32,512]{1,0:T(8,128)S(1)}, f32[32,512]{1,0:T(8,128)S(1)}, f32[32,512]{1,0:T(8,128)S...) custom-call(s32[2,4]{1,0:T(2,128)S(1)} %bitcast.31, f32[8,32,512]{2,1,0:T(8,128)S(1)} %place.1.base, ...), custom_call_target="tpu_custom_call" | custom-call | tf_op jit(solution)/shard_map/join/pallas_call | solution.py:178
  29.1 6.4 %collective-permute-start.10 = (f32[32,512]{1,0:T(8,128)S(1)}, f32[32,512]{1,0:T(8,128)S(1)}, u32[]{:S(2)}, u32[]{:S(2)}) collective-permute-start(f32[32,512]{1,0:T(8,128)S(1)} %get-tuple-element.24), channel_id=1, source_target_pairs={{0,192},{8,200},{16,208},{24,216},{32,224},{40,232},{48,240},{56,2... | collective-permute-start | bytes 196616 | tf_op jit(solution)/shard_map/ppermute | solution.py:191
  35.5 2.5 %collective-permute-start.14 = (f32[32,512]{1,0:T(8,128)S(1)}, f32[32,512]{1,0:T(8,128)S(1)}, u32[]{:S(2)}, u32[]{:S(2)}) collective-permute-start(f32[32,512]{1,0:T(8,128)S(1)} %get-tuple-element.32), channel_id=1, source_target_pairs={{0,96},{8,104},{16,112},{24,120},{32,128},{40,136},{48,144},{56,15... | collective-permute-start | bytes 196616 | tf_op jit(solution)/shard_map/ppermute | solution.py:191
  37.9 4.5 %collective-permute-start.15 = (f32[32,512]{1,0:T(8,128)S(1)}, f32[32,512]{1,0:T(8,128)S(1)}, u32[]{:S(2)}, u32[]{:S(2)}) collective-permute-start(f32[32,512]{1,0:T(8,128)S(1)} %get-tuple-element.33), channel_id=1, source_target_pairs={{0,128},{8,136},{16,144},{24,152},{32,160},{40,168},{48,176},{56,1... | collective-permute-start | bytes 196616 | tf_op jit(solution)/shard_map/ppermute | solution.py:191
  42.4 1.9 %collective-permute-start.16 = (f32[32,512]{1,0:T(8,128)S(1)}, f32[32,512]{1,0:T(8,128)S(1)}, u32[]{:S(2)}, u32[]{:S(2)}) collective-permute-start(f32[32,512]{1,0:T(8,128)S(1)} %get-tuple-element.34), channel_id=1, source_target_pairs={{0,160},{8,168},{16,176},{24,184},{32,192},{40,200},{48,208},{56,2... | collective-permute-start | bytes 196616 | tf_op jit(solution)/shard_map/ppermute | solution.py:191
  44.9 2.3 %collective-permute-done.12 = f32[32,512]{1,0:T(8,128)S(1)} collective-permute-done((f32[32,512]{1,0:T(8,128)S(1)}, f32[32,512]{1,0:T(8,128)S(1)}, u32[]{:S(2)}, u32[]{:S(2)}) %collective-permute-start.12) | collective-permute-done | bytes 65568 | tf_op jit(solution)/shard_map/ppermute | solution.py:191
  47.2 2.9 %collective-permute-start.13 = (f32[32,512]{1,0:T(8,128)S(1)}, f32[32,512]{1,0:T(8,128)S(1)}, u32[]{:S(2)}, u32[]{:S(2)}) collective-permute-start(f32[32,512]{1,0:T(8,128)S(1)} %get-tuple-element.30), channel_id=1, source_target_pairs={{0,32},{8,40},{16,48},{24,56},{32,64},{40,72},{48,80},{56,88},{64,... | collective-permute-start | bytes 196616 | tf_op jit(solution)/shard_map/ppermute | solution.py:191
  50.5 1.2 %collective-permute-done.17 = f32[32,512]{1,0:T(8,128)S(1)} collective-permute-done((f32[32,512]{1,0:T(8,128)S(1)}, f32[32,512]{1,0:T(8,128)S(1)}, u32[]{:S(2)}, u32[]{:S(2)}) %collective-permute-start.17) | collective-permute-done | bytes 65568 | tf_op jit(solution)/shard_map/ppermute | solution.py:191
  51.7 1.0 %collective-permute-done.13 = f32[32,512]{1,0:T(8,128)S(1)} collective-permute-done((f32[32,512]{1,0:T(8,128)S(1)}, f32[32,512]{1,0:T(8,128)S(1)}, u32[]{:S(2)}, u32[]{:S(2)}) %collective-permute-start.13) | collective-permute-done | bytes 65568 | tf_op jit(solution)/shard_map/ppermute | solution.py:191
  52.8 0.7 %copy.4 = f32[32,1,1,512]{3,2,1,0:T(1,128)} copy(f32[32,1,1,512]{3,0,2,1:T(8,128)S(1)} %fusion.9) | data formatting | bytes 131072 | tf_op jit(solution)/shard_map/reshape | solution.py:197
  (27 shorter events, 1.6 us)
Async XLA Ops:
  0.9 6.5 %collective-permute-start = (f32[32,512]{1,0:T(8,128)S(1)}, f32[32,512]{1,0:T(8,128)S(1)}, u32[]{:S(2)}, u32[]{:S(2)}) collective-permute-start(f32[32,512]{1,0:T(8,128)S(1)} %own.1.refs_0_), channel_id=1, source_target_pairs={{0,1},{1,0},{2,3},{3,2},{4,5},{5,4},{6,7},{7,6},{8,9},{9,8},{10,11... | collective-permute-start | bytes 196616 | tf_op jit(solution)/shard_map/ppermute | solution.py:139
  2.5 6.4 %collective-permute-start.5 = (f32[32,512]{1,0:T(8,128)S(1)}, f32[32,512]{1,0:T(8,128)S(1)}, u32[]{:S(2)}, u32[]{:S(2)}) collective-permute-start(f32[32,512]{1,0:T(8,128)S(1)} %own.1.refs_0_), channel_id=1, source_target_pairs={{0,6},{1,7},{2,0},{3,1},{4,2},{5,3},{6,4},{7,5},{8,14},{9,15},{10,... | collective-permute-start | bytes 196616 | tf_op jit(solution)/shard_map/ppermute | solution.py:143
  3.3 13.3 %collective-permute-start.3 = (f32[32,512]{1,0:T(8,128)S(1)}, f32[32,512]{1,0:T(8,128)S(1)}, u32[]{:S(2)}, u32[]{:S(2)}) collective-permute-start(f32[32,512]{1,0:T(8,128)S(1)} %own.1.refs_0_), channel_id=1, source_target_pairs={{0,4},{1,5},{2,6},{3,7},{4,0},{5,1},{6,2},{7,3},{8,12},{9,13},{10,... | collective-permute-start | bytes 196616 | tf_op jit(solution)/shard_map/ppermute | solution.py:143
  5.5 11.0 %collective-permute-start.1 = (f32[32,512]{1,0:T(8,128)S(1)}, f32[32,512]{1,0:T(8,128)S(1)}, u32[]{:S(2)}, u32[]{:S(2)}) collective-permute-start(f32[32,512]{1,0:T(8,128)S(1)} %own.1.refs_0_), channel_id=1, source_target_pairs={{0,2},{1,3},{2,4},{3,5},{4,6},{5,7},{6,0},{7,1},{8,10},{9,11},{10,... | collective-permute-start | bytes 196616 | tf_op jit(solution)/shard_map/ppermute | solution.py:143
  7.4 9.1 %collective-permute-start.6 = (f32[32,512]{1,0:T(8,128)S(1)}, f32[32,512]{1,0:T(8,128)S(1)}, u32[]{:S(2)}, u32[]{:S(2)}) collective-permute-start(f32[32,512]{1,0:T(8,128)S(1)} %collective-permute-done.refs_1_), channel_id=1, source_target_pairs={{0,6},{1,7},{2,0},{3,1},{4,2},{5,3},{6,4},{7,5},{8,14},{9,15},{10,... | collective-permute-start | bytes 196616 | tf_op jit(solution)/shard_map/ppermute | solution.py:143
  7.5 9.0 %collective-permute-start.4 = (f32[32,512]{1,0:T(8,128)S(1)}, f32[32,512]{1,0:T(8,128)S(1)}, u32[]{:S(2)}, u32[]{:S(2)}) collective-permute-start(f32[32,512]{1,0:T(8,128)S(1)} %collective-permute-done.refs_1_), channel_id=1, source_target_pairs={{0,4},{1,5},{2,6},{3,7},{4,0},{5,1},{6,2},{7,3},{8,12},{9,13},{10,... | collective-permute-start | bytes 196616 | tf_op jit(solution)/shard_map/ppermute | solution.py:143
  8.9 7.7 %collective-permute-start.2 = (f32[32,512]{1,0:T(8,128)S(1)}, f32[32,512]{1,0:T(8,128)S(1)}, u32[]{:S(2)}, u32[]{:S(2)}) collective-permute-start(f32[32,512]{1,0:T(8,128)S(1)} %collective-permute-done.refs_1_), channel_id=1, source_target_pairs={{0,2},{1,3},{2,4},{3,5},{4,6},{5,7},{6,0},{7,1},{8,10},{9,11},{10,... | collective-permute-start | bytes 196616 | tf_op jit(solution)/shard_map/ppermute | solution.py:143
  11.3 0.7 %copy-start = (s32[4,2]{0,1:T(2,128)S(1)}, s32[4,2]{0,1:T(2,128)}, u32[]{:S(2)}) copy-start(s32[4,2]{0,1:T(2,128)} %param.4) | copy-start | bytes 100
  16.5 11.2 %copy-start.1 = (s32[4,2]{0,1:T(2,128)S(1)}, s32[4,2]{0,1:T(2,128)}, u32[]{:S(2)}) copy-start(s32[4,2]{0,1:T(2,128)} %param.4) | copy-start | bytes 100
  18.6 8.1 %collective-permute-start.8 = (f32[136,512]{1,0:T(8,128)S(1)}, f32[136,512]{1,0:T(8,128)S(1)}, u32[]{:S(2)}, u32[]{:S(2)}) collective-permute-start(f32[136,512]{1,0:T(8,128)S(1)} %mirror.1.own), channel_id=1, source_target_pairs={{0,16},{8,24},{16,0},{24,8},{32,48},{40,56},{48,32},{56,40},{64,80... | collective-permute-start | bytes 835592 | tf_op jit(solution)/shard_map/ppermute | solution.py:165
  21.4 23.0 %all-to-all-start = ((f32[4,2,32,512]{3,2,1,0:T(8,128)}), f32[4,2,32,512]{3,2,1,0:T(8,128)S(1)}, u32[]{:S(2)}, u32[]{:S(2)}) async-start(f32[4,2,32,512]{3,2,1,0:T(8,128)} %get-tuple-element.21), calls=%async_computation | async-start | bytes 1048576 | tf_op jit(solution)/shard_map/all_to_all | solution.py:169
  26.1 1.6 %collective-permute-start.7 = (f32[136,512]{1,0:T(8,128)S(1)}, f32[136,512]{1,0:T(8,128)S(1)}, u32[]{:S(2)}, u32[]{:S(2)}) collective-permute-start(f32[136,512]{1,0:T(8,128)S(1)} %mirror.1.own), channel_id=1, source_target_pairs={{0,8},{8,0},{16,24},{24,16},{32,40},{40,32},{48,56},{56,48},{64,72... | collective-permute-start | bytes 835592 | tf_op jit(solution)/shard_map/ppermute | solution.py:166
  26.7 1.7 %collective-permute-start.9 = (f32[136,512]{1,0:T(8,128)S(1)}, f32[136,512]{1,0:T(8,128)S(1)}, u32[]{:S(2)}, u32[]{:S(2)}) collective-permute-start(f32[136,512]{1,0:T(8,128)S(1)} %collective-permute-done.8.one), channel_id=1, source_target_pairs={{0,8},{8,0},{16,24},{24,16},{32,40},{40,32},{48,56},{56,48},{64,72... | collective-permute-start | bytes 835592 | tf_op jit(solution)/shard_map/ppermute | solution.py:167
  29.1 15.3 %collective-permute-start.10 = (f32[32,512]{1,0:T(8,128)S(1)}, f32[32,512]{1,0:T(8,128)S(1)}, u32[]{:S(2)}, u32[]{:S(2)}) collective-permute-start(f32[32,512]{1,0:T(8,128)S(1)} %get-tuple-element.24), channel_id=1, source_target_pairs={{0,192},{8,200},{16,208},{24,216},{32,224},{40,232},{48,240},{56,2... | collective-permute-start | bytes 196616 | tf_op jit(solution)/shard_map/ppermute | solution.py:191
  35.5 11.7 %collective-permute-start.12 = (f32[32,512]{1,0:T(8,128)S(1)}, f32[32,512]{1,0:T(8,128)S(1)}, u32[]{:S(2)}, u32[]{:S(2)}) collective-permute-start(f32[32,512]{1,0:T(8,128)S(1)} %get-tuple-element.29), channel_id=1, source_target_pairs={{0,64},{8,72},{16,80},{24,88},{32,96},{40,104},{48,112},{56,120},{... | collective-permute-start | bytes 196616 | tf_op jit(solution)/shard_map/ppermute | solution.py:191
  35.5 11.7 %collective-permute-start.14 = (f32[32,512]{1,0:T(8,128)S(1)}, f32[32,512]{1,0:T(8,128)S(1)}, u32[]{:S(2)}, u32[]{:S(2)}) collective-permute-start(f32[32,512]{1,0:T(8,128)S(1)} %get-tuple-element.32), channel_id=1, source_target_pairs={{0,96},{8,104},{16,112},{24,120},{32,128},{40,136},{48,144},{56,15... | collective-permute-start | bytes 196616 | tf_op jit(solution)/shard_map/ppermute | solution.py:191
  37.9 12.2 %collective-permute-start.15 = (f32[32,512]{1,0:T(8,128)S(1)}, f32[32,512]{1,0:T(8,128)S(1)}, u32[]{:S(2)}, u32[]{:S(2)}) collective-permute-start(f32[32,512]{1,0:T(8,128)S(1)} %get-tuple-element.33), channel_id=1, source_target_pairs={{0,128},{8,136},{16,144},{24,152},{32,160},{40,168},{48,176},{56,1... | collective-permute-start | bytes 196616 | tf_op jit(solution)/shard_map/ppermute | solution.py:191
  42.4 8.0 %collective-permute-start.16 = (f32[32,512]{1,0:T(8,128)S(1)}, f32[32,512]{1,0:T(8,128)S(1)}, u32[]{:S(2)}, u32[]{:S(2)}) collective-permute-start(f32[32,512]{1,0:T(8,128)S(1)} %get-tuple-element.34), channel_id=1, source_target_pairs={{0,160},{8,168},{16,176},{24,184},{32,192},{40,200},{48,208},{56,2... | collective-permute-start | bytes 196616 | tf_op jit(solution)/shard_map/ppermute | solution.py:191
  44.5 6.0 %collective-permute-start.11 = (f32[32,512]{1,0:T(8,128)S(1)}, f32[32,512]{1,0:T(8,128)S(1)}, u32[]{:S(2)}, u32[]{:S(2)}) collective-permute-start(f32[32,512]{1,0:T(8,128)S(1)} %slice_bitcast_fusion), channel_id=1, source_target_pairs={{0,1},{1,0},{2,3},{3,2},{4,5},{5,4},{6,7},{7,6},{8,9},{9,8},{10,11... | collective-permute-start | bytes 196616 | tf_op jit(solution)/shard_map/ppermute | solution.py:194
  47.2 4.5 %collective-permute-start.17 = (f32[32,512]{1,0:T(8,128)S(1)}, f32[32,512]{1,0:T(8,128)S(1)}, u32[]{:S(2)}, u32[]{:S(2)}) collective-permute-start(f32[32,512]{1,0:T(8,128)S(1)} %get-tuple-element.36), channel_id=1, source_target_pairs={{0,224},{8,232},{16,240},{24,248},{32,0},{40,8},{48,16},{56,24},{6... | collective-permute-start | bytes 196616 | tf_op jit(solution)/shard_map/ppermute | solution.py:191
  47.2 5.5 %collective-permute-start.13 = (f32[32,512]{1,0:T(8,128)S(1)}, f32[32,512]{1,0:T(8,128)S(1)}, u32[]{:S(2)}, u32[]{:S(2)}) collective-permute-start(f32[32,512]{1,0:T(8,128)S(1)} %get-tuple-element.30), channel_id=1, source_target_pairs={{0,32},{8,40},{16,48},{24,56},{32,64},{40,72},{48,80},{56,88},{64,... | collective-permute-start | bytes 196616 | tf_op jit(solution)/shard_map/ppermute | solution.py:191

commit v5 on v4

--- a/solution.py
+++ b/solution.py
@@ -114,6 +114,15 @@
         out[...] = total[at]
 
 
+def total_kernel(*refs):
+    *parts, out = refs
+    total = parts[0][...]
+    for part in parts[1:]:
+        total = total + part[...]
+    for q in range(4):
+        out[:, q, :] = total[:, 128 * q:128 * (q + 1)]
+
+
 def shards(tiles, pairs, direction):
     k_count, width, _ = tiles.shape
     cols = direction.shape[0]
@@ -191,9 +200,15 @@
         parts[step] = lax.ppermute(parts[step], "grp", [(g, (g + 4 * step) % GRPS) for g in range(GRPS)])
     rows, parts[X_AFTER] = lax.optimization_barrier((rows, parts[X_AFTER]))
     row_sum = jnp.sum(rows, axis=0)
-    total = row_sum[0] + lax.ppermute(row_sum[1], "blk", x_swap)
-    for part in parts:
-        total = total + part
+    parts += [row_sum[0], lax.ppermute(row_sum[1], "blk", x_swap)]
+    total = pl.pallas_call(
+        total_kernel,
+        out_shape=jax.ShapeDtypeStruct((cols, 4, 128), f32),
+        in_specs=[vmem] * len(parts),
+        out_specs=vmem,
+        compiler_params=params,
+        name="total",
+    )(*parts)
     return total.reshape(cols, 1, 1, width)
 
 

time: 53.7 us -> 54.1 us (level)
  starting transfers between devices: 36.6 us -> 38.1 us
  waiting for transfers between devices: 6.39 us -> 5.45 us
  Pallas kernels: 8.81 us -> 9.57 us
  local copies, waits for them, and re-layouts: 1.39 us -> 0.7 us
    ppermute x7, waiting for transfers between devices: 4.82 us -> 1.85 us  [shards(): lax.ppermute(parts[step], 'grp', [(g, (g + 4 * step) % GRPS) for g in ran...]
    ppermute x1, waiting for transfers between devices: 0.01 us -> 2.03 us  [shards(): parts += [row_sum[0], lax.ppermute(row_sum[1], 'blk', x_swap)]]
    ppermute x7, starting transfers between devices: 18.3 us -> 19.7 us  [shards(): lax.ppermute(parts[step], 'grp', [(g, (g + 4 * step) % GRPS) for g in ran...]
    pallas_call x0 -> x1, Pallas kernels: none -> 0.7 us  [shards(): pl.pallas_call(total_kernel, out_shape=jax.ShapeDtypeStruct((cols, 4, 128...]
    reshape x1 -> x0, local copies, waits for them, and re-layouts: 0.7 us -> none  [shards(): return total.reshape(cols, 1, 1, width)]
where the time goes in v5:
time: 54.1 us; the launch traced here: 54 us
  starting transfers between devices  38.1 us (70%)
  Pallas kernels  9.57 us (18%)
  waiting for transfers between devices  5.45 us (10%)
  local copies, waits for them, and re-layouts  0.7 us (1%)
    ppermute x7, starting transfers between devices, shards(): lax.ppermute(parts[step], 'grp', [(g, (g + 4 * step) % GRPS) for g in ran...  19.7 us
    ppermute x6, starting transfers between devices, shards(): got += [lax.ppermute(own, 'blk', swap), lax.ppermute(near_own, 'blk', swap)]  8.79 us
    all_to_all x1, starting transfers between devices, shards(): lax.all_to_all(rows, 'blk', 0, 0, tiled=True, axis_index_groups=along_y)  4.71 us
    pallas_call x1, Pallas kernels, shards(): pl.pallas_call(rows_kernel, out_shape=[jax.ShapeDtypeStruct((YS, 2, cols,...  4.54 us
    ppermute x1, starting transfers between devices, shards(): over_x = lax.ppermute(terms, 'grp', [(g, g ^ 2) for g in range(GRPS)])  2.82 us
    ppermute x1, waiting for transfers between devices, shards(): parts += [row_sum[0], lax.ppermute(row_sum[1], 'blk', x_swap)]  2.03 us
    pallas_call x1, Pallas kernels, shards(): pl.pallas_call(mirror_kernel, out_shape=jax.ShapeDtypeStruct((k_count * c...  2 us
    ppermute x7, waiting for transfers between devices, shards(): lax.ppermute(parts[step], 'grp', [(g, (g + 4 * step) % GRPS) for g in ran...  1.85 us
  transfers between devices with their start and end apart: 19, of which 6 were waited for; matrix products, arithmetic and copies ran while one was open for 0% of the time, Pallas kernels for 11%

profile of v5, /device:TPU:8, one launch (start us, length us, event | category | flops | bytes accessed | tf_op | source)
XLA Modules:
  0.0 54.0 jit_solution(16279480380529651466)
XLA Ops:
  0.0 0.9 %own.1.refs_0_ = f32[32,512]{1,0:T(8,128)S(1)} custom-call(f32[32,32,4,128]{3,2,1,0:T(4,128)} %bitcast.11), custom_call_target="tpu_custom_call" | custom-call | tf_op jit(solution)/shard_map/own/pallas_call | solution.py:139
  0.9 1.6 %collective-permute-start = (f32[32,512]{1,0:T(8,128)S(1)}, f32[32,512]{1,0:T(8,128)S(1)}, u32[]{:S(2)}, u32[]{:S(2)}) collective-permute-start(f32[32,512]{1,0:T(8,128)S(1)} %own.1.refs_0_), channel_id=1, source_target_pairs={{0,1},{1,0},{2,3},{3,2},{4,5},{5,4},{6,7},{7,6},{8,9},{9,8},{10,11... | collective-permute-start | bytes 196616 | tf_op jit(solution)/shard_map/ppermute | solution.py:148
  2.5 0.8 %collective-permute-start.5 = (f32[32,512]{1,0:T(8,128)S(1)}, f32[32,512]{1,0:T(8,128)S(1)}, u32[]{:S(2)}, u32[]{:S(2)}) collective-permute-start(f32[32,512]{1,0:T(8,128)S(1)} %own.1.refs_0_), channel_id=1, source_target_pairs={{0,6},{1,7},{2,0},{3,1},{4,2},{5,3},{6,4},{7,5},{8,14},{9,15},{10,... | collective-permute-start | bytes 196616 | tf_op jit(solution)/shard_map/ppermute | solution.py:152
  3.3 2.3 %collective-permute-start.3 = (f32[32,512]{1,0:T(8,128)S(1)}, f32[32,512]{1,0:T(8,128)S(1)}, u32[]{:S(2)}, u32[]{:S(2)}) collective-permute-start(f32[32,512]{1,0:T(8,128)S(1)} %own.1.refs_0_), channel_id=1, source_target_pairs={{0,4},{1,5},{2,6},{3,7},{4,0},{5,1},{6,2},{7,3},{8,12},{9,13},{10,... | collective-permute-start | bytes 196616 | tf_op jit(solution)/shard_map/ppermute | solution.py:152
  5.5 1.9 %collective-permute-start.1 = (f32[32,512]{1,0:T(8,128)S(1)}, f32[32,512]{1,0:T(8,128)S(1)}, u32[]{:S(2)}, u32[]{:S(2)}) collective-permute-start(f32[32,512]{1,0:T(8,128)S(1)} %own.1.refs_0_), channel_id=1, source_target_pairs={{0,2},{1,3},{2,4},{3,5},{4,6},{5,7},{6,0},{7,1},{8,10},{9,11},{10,... | collective-permute-start | bytes 196616 | tf_op jit(solution)/shard_map/ppermute | solution.py:152
  7.5 1.3 %collective-permute-start.4 = (f32[32,512]{1,0:T(8,128)S(1)}, f32[32,512]{1,0:T(8,128)S(1)}, u32[]{:S(2)}, u32[]{:S(2)}) collective-permute-start(f32[32,512]{1,0:T(8,128)S(1)} %collective-permute-done.refs_1_), channel_id=1, source_target_pairs={{0,4},{1,5},{2,6},{3,7},{4,0},{5,1},{6,2},{7,3},{8,12},{9,13},{10,... | collective-permute-start | bytes 196616 | tf_op jit(solution)/shard_map/ppermute | solution.py:152
  8.9 2.4 %collective-permute-start.2 = (f32[32,512]{1,0:T(8,128)S(1)}, f32[32,512]{1,0:T(8,128)S(1)}, u32[]{:S(2)}, u32[]{:S(2)}) collective-permute-start(f32[32,512]{1,0:T(8,128)S(1)} %collective-permute-done.refs_1_), channel_id=1, source_target_pairs={{0,2},{1,3},{2,4},{3,5},{4,6},{5,7},{6,0},{7,1},{8,10},{9,11},{10,... | collective-permute-start | bytes 196616 | tf_op jit(solution)/shard_map/ppermute | solution.py:152
  12.0 4.5 %rows.1 = (f32[4,2,32,512]{3,2,1,0:T(8,128)}, f32[4,512,512]{2,1,0:T(8,128)S(1)}) custom-call(s32[2,4]{1,0:T(2,128)S(1)} %bitcast.7, f32[32,32,4,128]{3,2,1,0:T(4,128)} %bitcast.12, f32[4,512,512]{2,1,0:T(8,128)} %tiles.1), custom_call_target="tpu_custom_call" | custom-call | flops 600000000 | bytes 10000000 | tf_op jit(solution)/shard_map/rows/pallas_call | solution.py:154
  16.6 2.0 %mirror.1.own = f32[136,512]{1,0:T(8,128)S(1)} custom-call(s32[2,4]{1,0:T(2,128)S(1)} %bitcast.8, f32[32,512]{1,0:T(8,128)S(1)} %own.1.refs_0_, f32[32,512]{1,0:T(8,128)S(1)} %collective-permute-done.refs_1_, f32[32,512]{1,0:T(8,128)S(1)} %collective-permute-done.1.refs_2_, f32[32,512]{1,0:T(8,128)S(1)} %collective-permute-done.2.refs_3_, ...), custom_call_target="tpu_custom_call" | custom-call | tf_op jit(solution)/shard_map/mirror/pallas_call | solution.py:165
  18.6 2.8 %collective-permute-start.8 = (f32[136,512]{1,0:T(8,128)S(1)}, f32[136,512]{1,0:T(8,128)S(1)}, u32[]{:S(2)}, u32[]{:S(2)}) collective-permute-start(f32[136,512]{1,0:T(8,128)S(1)} %mirror.1.own), channel_id=1, source_target_pairs={{0,16},{8,24},{16,0},{24,8},{32,48},{40,56},{48,32},{56,40},{64,80... | collective-permute-start | bytes 835592 | tf_op jit(solution)/shard_map/ppermute | solution.py:174
  21.4 4.7 %all-to-all-start = ((f32[4,2,32,512]{3,2,1,0:T(8,128)}), f32[4,2,32,512]{3,2,1,0:T(8,128)S(1)}, u32[]{:S(2)}, u32[]{:S(2)}) async-start(f32[4,2,32,512]{3,2,1,0:T(8,128)} %get-tuple-element.30), calls=%async_computation | async-start | bytes 1048576 | tf_op jit(solution)/shard_map/all_to_all | solution.py:178
  26.7 1.0 %collective-permute-done.7.other = f32[136,512]{1,0:T(8,128)S(1)} collective-permute-done((f32[136,512]{1,0:T(8,128)S(1)}, f32[136,512]{1,0:T(8,128)S(1)}, u32[]{:S(2)}, u32[]{:S(2)}) %collective-permute-start.7) | collective-permute-done | bytes 278560 | tf_op jit(solution)/shard_map/ppermute | solution.py:175
  27.7 0.7 %place.1.base = f32[8,32,512]{2,1,0:T(8,128)S(1)} custom-call(s32[2,4]{1,0:T(2,128)S(1)} %bitcast.9, f32[136,512]{1,0:T(8,128)S(1)} %mirror.1.own, f32[136,512]{1,0:T(8,128)S(1)} %collective-permute-done.7.other), custom_call_target="tpu_custom_call" | custom-call | tf_op jit(solution)/shard_map/place/pallas_call | solution.py:179
  28.4 0.8 %join.1 = (f32[32,512]{1,0:T(8,128)S(1)}, f32[32,512]{1,0:T(8,128)S(1)}, f32[32,512]{1,0:T(8,128)S(1)}, f32[32,512]{1,0:T(8,128)S(1)}, f32[32,512]{1,0:T(8,128)S...) custom-call(s32[2,4]{1,0:T(2,128)S(1)} %bitcast.10, f32[8,32,512]{2,1,0:T(8,128)S(1)} %place.1.base, ...), custom_call_target="tpu_custom_call" | custom-call | tf_op jit(solution)/shard_map/join/pallas_call | solution.py:187
  29.1 3.3 %collective-permute-start.10 = (f32[32,512]{1,0:T(8,128)S(1)}, f32[32,512]{1,0:T(8,128)S(1)}, u32[]{:S(2)}, u32[]{:S(2)}) collective-permute-start(f32[32,512]{1,0:T(8,128)S(1)} %get-tuple-element.24), channel_id=1, source_target_pairs={{0,64},{8,72},{16,80},{24,88},{32,96},{40,104},{48,112},{56,120},{... | collective-permute-start | bytes 196616 | tf_op jit(solution)/shard_map/ppermute | solution.py:200
  32.4 3.2 %collective-permute-start.15 = (f32[32,512]{1,0:T(8,128)S(1)}, f32[32,512]{1,0:T(8,128)S(1)}, u32[]{:S(2)}, u32[]{:S(2)}) collective-permute-start(f32[32,512]{1,0:T(8,128)S(1)} %get-tuple-element.32), channel_id=1, source_target_pairs={{0,192},{8,200},{16,208},{24,216},{32,224},{40,232},{48,240},{56,2... | collective-permute-start | bytes 196616 | tf_op jit(solution)/shard_map/ppermute | solution.py:200
  35.6 1.8 %collective-permute-start.12 = (f32[32,512]{1,0:T(8,128)S(1)}, f32[32,512]{1,0:T(8,128)S(1)}, u32[]{:S(2)}, u32[]{:S(2)}) collective-permute-start(f32[32,512]{1,0:T(8,128)S(1)} %get-tuple-element.27), channel_id=1, source_target_pairs={{0,96},{8,104},{16,112},{24,120},{32,128},{40,136},{48,144},{56,15... | collective-permute-start | bytes 196616 | tf_op jit(solution)/shard_map/ppermute | solution.py:200
  37.4 3.8 %collective-permute-start.13 = (f32[32,512]{1,0:T(8,128)S(1)}, f32[32,512]{1,0:T(8,128)S(1)}, u32[]{:S(2)}, u32[]{:S(2)}) collective-permute-start(f32[32,512]{1,0:T(8,128)S(1)} %get-tuple-element.28), channel_id=1, source_target_pairs={{0,128},{8,136},{16,144},{24,152},{32,160},{40,168},{48,176},{56,1... | collective-permute-start | bytes 196616 | tf_op jit(solution)/shard_map/ppermute | solution.py:200
  41.2 4.4 %collective-permute-start.14 = (f32[32,512]{1,0:T(8,128)S(1)}, f32[32,512]{1,0:T(8,128)S(1)}, u32[]{:S(2)}, u32[]{:S(2)}) collective-permute-start(f32[32,512]{1,0:T(8,128)S(1)} %get-tuple-element.29), channel_id=1, source_target_pairs={{0,160},{8,168},{16,176},{24,184},{32,192},{40,200},{48,208},{56,2... | collective-permute-start | bytes 196616 | tf_op jit(solution)/shard_map/ppermute | solution.py:200
  45.6 1.0 %collective-permute-start.11 = (f32[32,512]{1,0:T(8,128)S(1)}, f32[32,512]{1,0:T(8,128)S(1)}, u32[]{:S(2)}, u32[]{:S(2)}) collective-permute-start(f32[32,512]{1,0:T(8,128)S(1)} %get-tuple-element.25), channel_id=1, source_target_pairs={{0,32},{8,40},{16,48},{24,56},{32,64},{40,72},{48,80},{56,88},{64,... | collective-permute-start | bytes 196616 | tf_op jit(solution)/shard_map/ppermute | solution.py:200
  46.6 2.2 %collective-permute-start.16 = (f32[32,512]{1,0:T(8,128)S(1)}, f32[32,512]{1,0:T(8,128)S(1)}, u32[]{:S(2)}, u32[]{:S(2)}) collective-permute-start(f32[32,512]{1,0:T(8,128)S(1)} %get-tuple-element.35), channel_id=1, source_target_pairs={{0,224},{8,232},{16,240},{24,248},{32,0},{40,8},{48,16},{56,24},{6... | collective-permute-start | bytes 196616 | tf_op jit(solution)/shard_map/ppermute | solution.py:200
  49.4 1.1 %collective-permute-done.14.refs_5_ = f32[32,512]{1,0:T(8,128)S(1)} collective-permute-done((f32[32,512]{1,0:T(8,128)S(1)}, f32[32,512]{1,0:T(8,128)S(1)}, u32[]{:S(2)}, u32[]{:S(2)}) %collective-permute-start.14) | collective-permute-done | bytes 65568 | tf_op jit(solution)/shard_map/ppermute | solution.py:200
  51.2 2.0 %collective-permute-done.17.refs_9_ = f32[32,512]{1,0:T(8,128)S(1)} collective-permute-done((f32[32,512]{1,0:T(8,128)S(1)}, f32[32,512]{1,0:T(8,128)S(1)}, u32[]{:S(2)}, u32[]{:S(2)}) %collective-permute-start.17) | collective-permute-done | bytes 65568 | tf_op jit(solution)/shard_map/ppermute | solution.py:203
  53.3 0.7 %total.1 = f32[32,4,128]{2,1,0:T(4,128)} custom-call(f32[32,512]{1,0:T(8,128)S(1)} %get-tuple-element.22.refs_0_, f32[32,512]{1,0:T(8,128)S(1)} %collective-permute-done.11.refs_1_, f32[32,512]{1,0:T(8,128)S(1)} %collective-permute-done.10.refs_2_, f32[32,512]{1,0:T(8,128)S(1)} %collective-permute-done.12.refs_3_, ...), custom_call_target="tpu_custom_call" | custom-call | tf_op jit(solution)/shard_map/total/pallas_call | solution.py:204
  (26 shorter events, 2.7 us)
Async XLA Ops:
  0.9 6.5 %collective-permute-start = (f32[32,512]{1,0:T(8,128)S(1)}, f32[32,512]{1,0:T(8,128)S(1)}, u32[]{:S(2)}, u32[]{:S(2)}) collective-permute-start(f32[32,512]{1,0:T(8,128)S(1)} %own.1.refs_0_), channel_id=1, source_target_pairs={{0,1},{1,0},{2,3},{3,2},{4,5},{5,4},{6,7},{7,6},{8,9},{9,8},{10,11... | collective-permute-start | bytes 196616 | tf_op jit(solution)/shard_map/ppermute | solution.py:148
  2.5 6.4 %collective-permute-start.5 = (f32[32,512]{1,0:T(8,128)S(1)}, f32[32,512]{1,0:T(8,128)S(1)}, u32[]{:S(2)}, u32[]{:S(2)}) collective-permute-start(f32[32,512]{1,0:T(8,128)S(1)} %own.1.refs_0_), channel_id=1, source_target_pairs={{0,6},{1,7},{2,0},{3,1},{4,2},{5,3},{6,4},{7,5},{8,14},{9,15},{10,... | collective-permute-start | bytes 196616 | tf_op jit(solution)/shard_map/ppermute | solution.py:152
  3.3 13.3 %collective-permute-start.3 = (f32[32,512]{1,0:T(8,128)S(1)}, f32[32,512]{1,0:T(8,128)S(1)}, u32[]{:S(2)}, u32[]{:S(2)}) collective-permute-start(f32[32,512]{1,0:T(8,128)S(1)} %own.1.refs_0_), channel_id=1, source_target_pairs={{0,4},{1,5},{2,6},{3,7},{4,0},{5,1},{6,2},{7,3},{8,12},{9,13},{10,... | collective-permute-start | bytes 196616 | tf_op jit(solution)/shard_map/ppermute | solution.py:152
  5.5 11.0 %collective-permute-start.1 = (f32[32,512]{1,0:T(8,128)S(1)}, f32[32,512]{1,0:T(8,128)S(1)}, u32[]{:S(2)}, u32[]{:S(2)}) collective-permute-start(f32[32,512]{1,0:T(8,128)S(1)} %own.1.refs_0_), channel_id=1, source_target_pairs={{0,2},{1,3},{2,4},{3,5},{4,6},{5,7},{6,0},{7,1},{8,10},{9,11},{10,... | collective-permute-start | bytes 196616 | tf_op jit(solution)/shard_map/ppermute | solution.py:152
  7.4 9.1 %collective-permute-start.6 = (f32[32,512]{1,0:T(8,128)S(1)}, f32[32,512]{1,0:T(8,128)S(1)}, u32[]{:S(2)}, u32[]{:S(2)}) collective-permute-start(f32[32,512]{1,0:T(8,128)S(1)} %collective-permute-done.refs_1_), channel_id=1, source_target_pairs={{0,6},{1,7},{2,0},{3,1},{4,2},{5,3},{6,4},{7,5},{8,14},{9,15},{10,... | collective-permute-start | bytes 196616 | tf_op jit(solution)/shard_map/ppermute | solution.py:152
  7.5 9.0 %collective-permute-start.4 = (f32[32,512]{1,0:T(8,128)S(1)}, f32[32,512]{1,0:T(8,128)S(1)}, u32[]{:S(2)}, u32[]{:S(2)}) collective-permute-start(f32[32,512]{1,0:T(8,128)S(1)} %collective-permute-done.refs_1_), channel_id=1, source_target_pairs={{0,4},{1,5},{2,6},{3,7},{4,0},{5,1},{6,2},{7,3},{8,12},{9,13},{10,... | collective-permute-start | bytes 196616 | tf_op jit(solution)/shard_map/ppermute | solution.py:152
  8.9 7.7 %collective-permute-start.2 = (f32[32,512]{1,0:T(8,128)S(1)}, f32[32,512]{1,0:T(8,128)S(1)}, u32[]{:S(2)}, u32[]{:S(2)}) collective-permute-start(f32[32,512]{1,0:T(8,128)S(1)} %collective-permute-done.refs_1_), channel_id=1, source_target_pairs={{0,2},{1,3},{2,4},{3,5},{4,6},{5,7},{6,0},{7,1},{8,10},{9,11},{10,... | collective-permute-start | bytes 196616 | tf_op jit(solution)/shard_map/ppermute | solution.py:152
  11.3 0.7 %copy-start = (s32[4,2]{0,1:T(2,128)S(1)}, s32[4,2]{0,1:T(2,128)}, u32[]{:S(2)}) copy-start(s32[4,2]{0,1:T(2,128)} %param.4) | copy-start | bytes 100
  16.5 11.2 %copy-start.1 = (s32[4,2]{0,1:T(2,128)S(1)}, s32[4,2]{0,1:T(2,128)}, u32[]{:S(2)}) copy-start(s32[4,2]{0,1:T(2,128)} %param.4) | copy-start | bytes 100
  18.6 8.1 %collective-permute-start.8 = (f32[136,512]{1,0:T(8,128)S(1)}, f32[136,512]{1,0:T(8,128)S(1)}, u32[]{:S(2)}, u32[]{:S(2)}) collective-permute-start(f32[136,512]{1,0:T(8,128)S(1)} %mirror.1.own), channel_id=1, source_target_pairs={{0,16},{8,24},{16,0},{24,8},{32,48},{40,56},{48,32},{56,40},{64,80... | collective-permute-start | bytes 835592 | tf_op jit(solution)/shard_map/ppermute | solution.py:174
  21.4 25.2 %all-to-all-start = ((f32[4,2,32,512]{3,2,1,0:T(8,128)}), f32[4,2,32,512]{3,2,1,0:T(8,128)S(1)}, u32[]{:S(2)}, u32[]{:S(2)}) async-start(f32[4,2,32,512]{3,2,1,0:T(8,128)} %get-tuple-element.30), calls=%async_computation | async-start | bytes 1048576 | tf_op jit(solution)/shard_map/all_to_all | solution.py:178
  26.1 1.6 %collective-permute-start.7 = (f32[136,512]{1,0:T(8,128)S(1)}, f32[136,512]{1,0:T(8,128)S(1)}, u32[]{:S(2)}, u32[]{:S(2)}) collective-permute-start(f32[136,512]{1,0:T(8,128)S(1)} %mirror.1.own), channel_id=1, source_target_pairs={{0,8},{8,0},{16,24},{24,16},{32,40},{40,32},{48,56},{56,48},{64,72... | collective-permute-start | bytes 835592 | tf_op jit(solution)/shard_map/ppermute | solution.py:175
  26.7 1.7 %collective-permute-start.9 = (f32[136,512]{1,0:T(8,128)S(1)}, f32[136,512]{1,0:T(8,128)S(1)}, u32[]{:S(2)}, u32[]{:S(2)}) collective-permute-start(f32[136,512]{1,0:T(8,128)S(1)} %collective-permute-done.8.one), channel_id=1, source_target_pairs={{0,8},{8,0},{16,24},{24,16},{32,40},{40,32},{48,56},{56,48},{64,72... | collective-permute-start | bytes 835592 | tf_op jit(solution)/shard_map/ppermute | solution.py:176
  29.1 16.4 %collective-permute-start.10 = (f32[32,512]{1,0:T(8,128)S(1)}, f32[32,512]{1,0:T(8,128)S(1)}, u32[]{:S(2)}, u32[]{:S(2)}) collective-permute-start(f32[32,512]{1,0:T(8,128)S(1)} %get-tuple-element.24), channel_id=1, source_target_pairs={{0,64},{8,72},{16,80},{24,88},{32,96},{40,104},{48,112},{56,120},{... | collective-permute-start | bytes 196616 | tf_op jit(solution)/shard_map/ppermute | solution.py:200
  32.4 14.2 %collective-permute-start.15 = (f32[32,512]{1,0:T(8,128)S(1)}, f32[32,512]{1,0:T(8,128)S(1)}, u32[]{:S(2)}, u32[]{:S(2)}) collective-permute-start(f32[32,512]{1,0:T(8,128)S(1)} %get-tuple-element.32), channel_id=1, source_target_pairs={{0,192},{8,200},{16,208},{24,216},{32,224},{40,232},{48,240},{56,2... | collective-permute-start | bytes 196616 | tf_op jit(solution)/shard_map/ppermute | solution.py:200
  35.6 13.3 %collective-permute-start.12 = (f32[32,512]{1,0:T(8,128)S(1)}, f32[32,512]{1,0:T(8,128)S(1)}, u32[]{:S(2)}, u32[]{:S(2)}) collective-permute-start(f32[32,512]{1,0:T(8,128)S(1)} %get-tuple-element.27), channel_id=1, source_target_pairs={{0,96},{8,104},{16,112},{24,120},{32,128},{40,136},{48,144},{56,15... | collective-permute-start | bytes 196616 | tf_op jit(solution)/shard_map/ppermute | solution.py:200
  37.4 12.0 %collective-permute-start.13 = (f32[32,512]{1,0:T(8,128)S(1)}, f32[32,512]{1,0:T(8,128)S(1)}, u32[]{:S(2)}, u32[]{:S(2)}) collective-permute-start(f32[32,512]{1,0:T(8,128)S(1)} %get-tuple-element.28), channel_id=1, source_target_pairs={{0,128},{8,136},{16,144},{24,152},{32,160},{40,168},{48,176},{56,1... | collective-permute-start | bytes 196616 | tf_op jit(solution)/shard_map/ppermute | solution.py:200
  41.2 9.2 %collective-permute-start.14 = (f32[32,512]{1,0:T(8,128)S(1)}, f32[32,512]{1,0:T(8,128)S(1)}, u32[]{:S(2)}, u32[]{:S(2)}) collective-permute-start(f32[32,512]{1,0:T(8,128)S(1)} %get-tuple-element.29), channel_id=1, source_target_pairs={{0,160},{8,168},{16,176},{24,184},{32,192},{40,200},{48,208},{56,2... | collective-permute-start | bytes 196616 | tf_op jit(solution)/shard_map/ppermute | solution.py:200
  45.6 5.5 %collective-permute-start.11 = (f32[32,512]{1,0:T(8,128)S(1)}, f32[32,512]{1,0:T(8,128)S(1)}, u32[]{:S(2)}, u32[]{:S(2)}) collective-permute-start(f32[32,512]{1,0:T(8,128)S(1)} %get-tuple-element.25), channel_id=1, source_target_pairs={{0,32},{8,40},{16,48},{24,56},{32,64},{40,72},{48,80},{56,88},{64,... | collective-permute-start | bytes 196616 | tf_op jit(solution)/shard_map/ppermute | solution.py:200
  46.6 4.6 %collective-permute-start.16 = (f32[32,512]{1,0:T(8,128)S(1)}, f32[32,512]{1,0:T(8,128)S(1)}, u32[]{:S(2)}, u32[]{:S(2)}) collective-permute-start(f32[32,512]{1,0:T(8,128)S(1)} %get-tuple-element.35), channel_id=1, source_target_pairs={{0,224},{8,232},{16,240},{24,248},{32,0},{40,8},{48,16},{56,24},{6... | collective-permute-start | bytes 196616 | tf_op jit(solution)/shard_map/ppermute | solution.py:200
  48.9 4.4 %collective-permute-start.17 = (f32[32,512]{1,0:T(8,128)S(1)}, f32[32,512]{1,0:T(8,128)S(1)}, u32[]{:S(2)}, u32[]{:S(2)}) collective-permute-start(f32[32,512]{1,0:T(8,128)S(1)} %get-tuple-element.37), channel_id=1, source_target_pairs={{0,1},{1,0},{2,3},{3,2},{4,5},{5,4},{6,7},{7,6},{8,9},{9,8},{10,11... | collective-permute-start | bytes 196616 | tf_op jit(solution)/shard_map/ppermute | solution.py:203

commit v6 on v4

--- a/solution.py
+++ b/solution.py
@@ -11,7 +11,7 @@
 YS = 4
 Z_ORDER = (4, 3, 5, 2, 6, 1, 7)
 Z_AFTER = {1: 2, 7: 6}
-X_AFTER = 6
+X_AFTER = 2
 VMEM_BYTES = 32 * 1024 * 1024
 
 

time: 53.7 us -> 59.3 us (1.10)
  waiting for transfers between devices: 6.39 us -> 10.5 us
  starting transfers between devices: 36.6 us -> 38.1 us
    ppermute x7, waiting for transfers between devices: 4.82 us -> 8.95 us  [shards(): lax.ppermute(parts[step], 'grp', [(g, (g + 4 * step) % GRPS) for g in ran...]
    ppermute x7, starting transfers between devices: 18.3 us -> 19.7 us  [shards(): lax.ppermute(parts[step], 'grp', [(g, (g + 4 * step) % GRPS) for g in ran...]
  transfers between devices with their start and end apart: 19 -> 19, of which waited for: 6 -> 4; matrix products, arithmetic and copies ran while one was open for 0% -> 0% of each run, Pallas kernels for 11% -> 10%
where the time goes in v6:
time: 59.3 us; the launch traced here: 59 us
  starting transfers between devices  38.1 us (64%)
  waiting for transfers between devices  10.5 us (18%)
  Pallas kernels  8.84 us (15%)
  local copies, waits for them, and re-layouts  1.39 us (2%)
    ppermute x7, starting transfers between devices, shards(): lax.ppermute(parts[step], 'grp', [(g, (g + 4 * step) % GRPS) for g in ran...  19.7 us
    ppermute x7, waiting for transfers between devices, shards(): lax.ppermute(parts[step], 'grp', [(g, (g + 4 * step) % GRPS) for g in ran...  8.95 us
    ppermute x6, starting transfers between devices, shards(): got += [lax.ppermute(own, 'blk', swap), lax.ppermute(near_own, 'blk', swap)]  8.79 us
    all_to_all x1, starting transfers between devices, shards(): lax.all_to_all(rows, 'blk', 0, 0, tiled=True, axis_index_groups=along_y)  4.74 us
    pallas_call x1, Pallas kernels, shards(): pl.pallas_call(rows_kernel, out_shape=[jax.ShapeDtypeStruct((YS, 2, cols,...  4.53 us
    ppermute x1, starting transfers between devices, shards(): over_x = lax.ppermute(terms, 'grp', [(g, g ^ 2) for g in range(GRPS)])  2.8 us
    pallas_call x1, Pallas kernels, shards(): pl.pallas_call(mirror_kernel, out_shape=jax.ShapeDtypeStruct((k_count * c...  1.98 us
    ppermute x1, starting transfers between devices, shards(): near_own = lax.ppermute(own, 'blk', x_swap)  1.58 us
  transfers between devices with their start and end apart: 19, of which 4 were waited for; matrix products, arithmetic and copies ran while one was open for 0% of the time, Pallas kernels for 10%

profile of v6, /device:TPU:8, one launch (start us, length us, event | category | flops | bytes accessed | tf_op | source)
XLA Modules:
  0.0 59.0 jit_solution(17131991574334037992)
XLA Ops:
  0.0 0.9 %own.1.refs_0_ = f32[32,512]{1,0:T(8,128)S(1)} custom-call(f32[32,32,4,128]{3,2,1,0:T(4,128)} %bitcast.32), custom_call_target="tpu_custom_call" | custom-call | tf_op jit(solution)/shard_map/own/pallas_call | solution.py:130
  0.9 1.6 %collective-permute-start = (f32[32,512]{1,0:T(8,128)S(1)}, f32[32,512]{1,0:T(8,128)S(1)}, u32[]{:S(2)}, u32[]{:S(2)}) collective-permute-start(f32[32,512]{1,0:T(8,128)S(1)} %own.1.refs_0_), channel_id=1, source_target_pairs={{0,1},{1,0},{2,3},{3,2},{4,5},{5,4},{6,7},{7,6},{8,9},{9,8},{10,11... | collective-permute-start | bytes 196616 | tf_op jit(solution)/shard_map/ppermute | solution.py:139
  2.5 0.8 %collective-permute-start.5 = (f32[32,512]{1,0:T(8,128)S(1)}, f32[32,512]{1,0:T(8,128)S(1)}, u32[]{:S(2)}, u32[]{:S(2)}) collective-permute-start(f32[32,512]{1,0:T(8,128)S(1)} %own.1.refs_0_), channel_id=1, source_target_pairs={{0,6},{1,7},{2,0},{3,1},{4,2},{5,3},{6,4},{7,5},{8,14},{9,15},{10,... | collective-permute-start | bytes 196616 | tf_op jit(solution)/shard_map/ppermute | solution.py:143
  3.3 2.3 %collective-permute-start.3 = (f32[32,512]{1,0:T(8,128)S(1)}, f32[32,512]{1,0:T(8,128)S(1)}, u32[]{:S(2)}, u32[]{:S(2)}) collective-permute-start(f32[32,512]{1,0:T(8,128)S(1)} %own.1.refs_0_), channel_id=1, source_target_pairs={{0,4},{1,5},{2,6},{3,7},{4,0},{5,1},{6,2},{7,3},{8,12},{9,13},{10,... | collective-permute-start | bytes 196616 | tf_op jit(solution)/shard_map/ppermute | solution.py:143
  5.5 1.9 %collective-permute-start.1 = (f32[32,512]{1,0:T(8,128)S(1)}, f32[32,512]{1,0:T(8,128)S(1)}, u32[]{:S(2)}, u32[]{:S(2)}) collective-permute-start(f32[32,512]{1,0:T(8,128)S(1)} %own.1.refs_0_), channel_id=1, source_target_pairs={{0,2},{1,3},{2,4},{3,5},{4,6},{5,7},{6,0},{7,1},{8,10},{9,11},{10,... | collective-permute-start | bytes 196616 | tf_op jit(solution)/shard_map/ppermute | solution.py:143
  7.5 1.3 %collective-permute-start.4 = (f32[32,512]{1,0:T(8,128)S(1)}, f32[32,512]{1,0:T(8,128)S(1)}, u32[]{:S(2)}, u32[]{:S(2)}) collective-permute-start(f32[32,512]{1,0:T(8,128)S(1)} %collective-permute-done.refs_1_), channel_id=1, source_target_pairs={{0,4},{1,5},{2,6},{3,7},{4,0},{5,1},{6,2},{7,3},{8,12},{9,13},{10,... | collective-permute-start | bytes 196616 | tf_op jit(solution)/shard_map/ppermute | solution.py:143
  8.9 2.4 %collective-permute-start.2 = (f32[32,512]{1,0:T(8,128)S(1)}, f32[32,512]{1,0:T(8,128)S(1)}, u32[]{:S(2)}, u32[]{:S(2)}) collective-permute-start(f32[32,512]{1,0:T(8,128)S(1)} %collective-permute-done.refs_1_), channel_id=1, source_target_pairs={{0,2},{1,3},{2,4},{3,5},{4,6},{5,7},{6,0},{7,1},{8,10},{9,11},{10,... | collective-permute-start | bytes 196616 | tf_op jit(solution)/shard_map/ppermute | solution.py:143
  11.3 0.7 %copy-done = s32[4,2]{0,1:T(2,128)S(1)} copy-done((s32[4,2]{0,1:T(2,128)S(1)}, s32[4,2]{0,1:T(2,128)}, u32[]{:S(2)}) %copy-start) | copy-done | bytes 56
  12.0 4.5 %rows.1 = (f32[4,2,32,512]{3,2,1,0:T(8,128)}, f32[4,512,512]{2,1,0:T(8,128)S(1)}) custom-call(s32[2,4]{1,0:T(2,128)S(1)} %bitcast.28, f32[32,32,4,128]{3,2,1,0:T(4,128)} %bitcast.33, f32[4,512,512]{2,1,0:T(8,128)} %tiles.1), custom_call_target="tpu_custom_call" | custom-call | flops 600000000 | bytes 10000000 | tf_op jit(solution)/shard_map/rows/pallas_call | solution.py:145
  16.6 2.0 %mirror.1.own = f32[136,512]{1,0:T(8,128)S(1)} custom-call(s32[2,4]{1,0:T(2,128)S(1)} %bitcast.29, f32[32,512]{1,0:T(8,128)S(1)} %own.1.refs_0_, f32[32,512]{1,0:T(8,128)S(1)} %collective-permute-done.refs_1_, f32[32,512]{1,0:T(8,128)S(1)} %collective-permute-done.1.refs_2_, f32[32,512]{1,0:T(8,128)S(1)} %collective-permute-done.2.refs_3_, ...), custom_call_target="tpu_custom_call" | custom-call | tf_op jit(solution)/shard_map/mirror/pallas_call | solution.py:156
  18.5 2.8 %collective-permute-start.8 = (f32[136,512]{1,0:T(8,128)S(1)}, f32[136,512]{1,0:T(8,128)S(1)}, u32[]{:S(2)}, u32[]{:S(2)}) collective-permute-start(f32[136,512]{1,0:T(8,128)S(1)} %mirror.1.own), channel_id=1, source_target_pairs={{0,16},{8,24},{16,0},{24,8},{32,48},{40,56},{48,32},{56,40},{64,80... | collective-permute-start | bytes 835592 | tf_op jit(solution)/shard_map/ppermute | solution.py:165
  21.3 4.7 %all-to-all-start = ((f32[4,2,32,512]{3,2,1,0:T(8,128)}), f32[4,2,32,512]{3,2,1,0:T(8,128)S(1)}, u32[]{:S(2)}, u32[]{:S(2)}) async-start(f32[4,2,32,512]{3,2,1,0:T(8,128)} %get-tuple-element.21), calls=%async_computation | async-start | bytes 1048576 | tf_op jit(solution)/shard_map/all_to_all | solution.py:169
  26.7 1.0 %collective-permute-done.7.other = f32[136,512]{1,0:T(8,128)S(1)} collective-permute-done((f32[136,512]{1,0:T(8,128)S(1)}, f32[136,512]{1,0:T(8,128)S(1)}, u32[]{:S(2)}, u32[]{:S(2)}) %collective-permute-start.7) | collective-permute-done | bytes 278560 | tf_op jit(solution)/shard_map/ppermute | solution.py:166
  27.7 0.7 %place.1.base = f32[8,32,512]{2,1,0:T(8,128)S(1)} custom-call(s32[2,4]{1,0:T(2,128)S(1)} %bitcast.30, f32[136,512]{1,0:T(8,128)S(1)} %mirror.1.own, f32[136,512]{1,0:T(8,128)S(1)} %collective-permute-done.7.other), custom_call_target="tpu_custom_call" | custom-call | tf_op jit(solution)/shard_map/place/pallas_call | solution.py:170
  28.4 0.7 %join.1 = (f32[32,512]{1,0:T(8,128)S(1)}, f32[32,512]{1,0:T(8,128)S(1)}, f32[32,512]{1,0:T(8,128)S(1)}, f32[32,512]{1,0:T(8,128)S(1)}, f32[32,512]{1,0:T(8,128)S...) custom-call(s32[2,4]{1,0:T(2,128)S(1)} %bitcast.31, f32[8,32,512]{2,1,0:T(8,128)S(1)} %place.1.base, ...), custom_call_target="tpu_custom_call" | custom-call | tf_op jit(solution)/shard_map/join/pallas_call | solution.py:178
  29.1 3.4 %collective-permute-start.10 = (f32[32,512]{1,0:T(8,128)S(1)}, f32[32,512]{1,0:T(8,128)S(1)}, u32[]{:S(2)}, u32[]{:S(2)}) collective-permute-start(f32[32,512]{1,0:T(8,128)S(1)} %get-tuple-element.24), channel_id=1, source_target_pairs={{0,64},{8,72},{16,80},{24,88},{32,96},{40,104},{48,112},{56,120},{... | collective-permute-start | bytes 196616 | tf_op jit(solution)/shard_map/ppermute | solution.py:191
  32.5 4.9 %collective-permute-start.13 = (f32[32,512]{1,0:T(8,128)S(1)}, f32[32,512]{1,0:T(8,128)S(1)}, u32[]{:S(2)}, u32[]{:S(2)}) collective-permute-start(f32[32,512]{1,0:T(8,128)S(1)} %get-tuple-element.30), channel_id=1, source_target_pairs={{0,96},{8,104},{16,112},{24,120},{32,128},{40,136},{48,144},{56,15... | collective-permute-start | bytes 196616 | tf_op jit(solution)/shard_map/ppermute | solution.py:191
  37.4 1.0 %collective-permute-start.14 = (f32[32,512]{1,0:T(8,128)S(1)}, f32[32,512]{1,0:T(8,128)S(1)}, u32[]{:S(2)}, u32[]{:S(2)}) collective-permute-start(f32[32,512]{1,0:T(8,128)S(1)} %get-tuple-element.31), channel_id=1, source_target_pairs={{0,128},{8,136},{16,144},{24,152},{32,160},{40,168},{48,176},{56,1... | collective-permute-start | bytes 196616 | tf_op jit(solution)/shard_map/ppermute | solution.py:191
  38.4 4.5 %collective-permute-start.15 = (f32[32,512]{1,0:T(8,128)S(1)}, f32[32,512]{1,0:T(8,128)S(1)}, u32[]{:S(2)}, u32[]{:S(2)}) collective-permute-start(f32[32,512]{1,0:T(8,128)S(1)} %get-tuple-element.32), channel_id=1, source_target_pairs={{0,160},{8,168},{16,176},{24,184},{32,192},{40,200},{48,208},{56,2... | collective-permute-start | bytes 196616 | tf_op jit(solution)/shard_map/ppermute | solution.py:191
  42.9 2.7 %collective-permute-start.16 = (f32[32,512]{1,0:T(8,128)S(1)}, f32[32,512]{1,0:T(8,128)S(1)}, u32[]{:S(2)}, u32[]{:S(2)}) collective-permute-start(f32[32,512]{1,0:T(8,128)S(1)} %get-tuple-element.34), channel_id=1, source_target_pairs={{0,192},{8,200},{16,208},{24,216},{32,224},{40,232},{48,240},{56,2... | collective-permute-start | bytes 196616 | tf_op jit(solution)/shard_map/ppermute | solution.py:191
  46.1 6.7 %collective-permute-done.16 = f32[32,512]{1,0:T(8,128)S(1)} collective-permute-done((f32[32,512]{1,0:T(8,128)S(1)}, f32[32,512]{1,0:T(8,128)S(1)}, u32[]{:S(2)}, u32[]{:S(2)}) %collective-permute-start.16) | collective-permute-done | bytes 65568 | tf_op jit(solution)/shard_map/ppermute | solution.py:191
  53.4 2.6 %collective-permute-start.17 = (f32[32,512]{1,0:T(8,128)S(1)}, f32[32,512]{1,0:T(8,128)S(1)}, u32[]{:S(2)}, u32[]{:S(2)}) collective-permute-start(f32[32,512]{1,0:T(8,128)S(1)} %get-tuple-element.36), channel_id=1, source_target_pairs={{0,224},{8,232},{16,240},{24,248},{32,0},{40,8},{48,16},{56,24},{6... | collective-permute-start | bytes 196616 | tf_op jit(solution)/shard_map/ppermute | solution.py:191
  56.1 2.2 %collective-permute-done.12 = f32[32,512]{1,0:T(8,128)S(1)} collective-permute-done((f32[32,512]{1,0:T(8,128)S(1)}, f32[32,512]{1,0:T(8,128)S(1)}, u32[]{:S(2)}, u32[]{:S(2)}) %collective-permute-start.12) | collective-permute-done | bytes 65568 | tf_op jit(solution)/shard_map/ppermute | solution.py:191
  58.3 0.7 %copy.4 = f32[32,1,1,512]{3,2,1,0:T(1,128)} copy(f32[32,1,1,512]{3,0,2,1:T(8,128)S(1)} %fusion.9) | data formatting | bytes 131072 | tf_op jit(solution)/shard_map/reshape | solution.py:197
  (27 shorter events, 2.0 us)
Async XLA Ops:
  0.9 6.5 %collective-permute-start = (f32[32,512]{1,0:T(8,128)S(1)}, f32[32,512]{1,0:T(8,128)S(1)}, u32[]{:S(2)}, u32[]{:S(2)}) collective-permute-start(f32[32,512]{1,0:T(8,128)S(1)} %own.1.refs_0_), channel_id=1, source_target_pairs={{0,1},{1,0},{2,3},{3,2},{4,5},{5,4},{6,7},{7,6},{8,9},{9,8},{10,11... | collective-permute-start | bytes 196616 | tf_op jit(solution)/shard_map/ppermute | solution.py:139
  2.5 6.4 %collective-permute-start.5 = (f32[32,512]{1,0:T(8,128)S(1)}, f32[32,512]{1,0:T(8,128)S(1)}, u32[]{:S(2)}, u32[]{:S(2)}) collective-permute-start(f32[32,512]{1,0:T(8,128)S(1)} %own.1.refs_0_), channel_id=1, source_target_pairs={{0,6},{1,7},{2,0},{3,1},{4,2},{5,3},{6,4},{7,5},{8,14},{9,15},{10,... | collective-permute-start | bytes 196616 | tf_op jit(solution)/shard_map/ppermute | solution.py:143
  3.3 13.3 %collective-permute-start.3 = (f32[32,512]{1,0:T(8,128)S(1)}, f32[32,512]{1,0:T(8,128)S(1)}, u32[]{:S(2)}, u32[]{:S(2)}) collective-permute-start(f32[32,512]{1,0:T(8,128)S(1)} %own.1.refs_0_), channel_id=1, source_target_pairs={{0,4},{1,5},{2,6},{3,7},{4,0},{5,1},{6,2},{7,3},{8,12},{9,13},{10,... | collective-permute-start | bytes 196616 | tf_op jit(solution)/shard_map/ppermute | solution.py:143
  5.5 11.0 %collective-permute-start.1 = (f32[32,512]{1,0:T(8,128)S(1)}, f32[32,512]{1,0:T(8,128)S(1)}, u32[]{:S(2)}, u32[]{:S(2)}) collective-permute-start(f32[32,512]{1,0:T(8,128)S(1)} %own.1.refs_0_), channel_id=1, source_target_pairs={{0,2},{1,3},{2,4},{3,5},{4,6},{5,7},{6,0},{7,1},{8,10},{9,11},{10,... | collective-permute-start | bytes 196616 | tf_op jit(solution)/shard_map/ppermute | solution.py:143
  7.4 9.1 %collective-permute-start.6 = (f32[32,512]{1,0:T(8,128)S(1)}, f32[32,512]{1,0:T(8,128)S(1)}, u32[]{:S(2)}, u32[]{:S(2)}) collective-permute-start(f32[32,512]{1,0:T(8,128)S(1)} %collective-permute-done.refs_1_), channel_id=1, source_target_pairs={{0,6},{1,7},{2,0},{3,1},{4,2},{5,3},{6,4},{7,5},{8,14},{9,15},{10,... | collective-permute-start | bytes 196616 | tf_op jit(solution)/shard_map/ppermute | solution.py:143
  7.5 9.0 %collective-permute-start.4 = (f32[32,512]{1,0:T(8,128)S(1)}, f32[32,512]{1,0:T(8,128)S(1)}, u32[]{:S(2)}, u32[]{:S(2)}) collective-permute-start(f32[32,512]{1,0:T(8,128)S(1)} %collective-permute-done.refs_1_), channel_id=1, source_target_pairs={{0,4},{1,5},{2,6},{3,7},{4,0},{5,1},{6,2},{7,3},{8,12},{9,13},{10,... | collective-permute-start | bytes 196616 | tf_op jit(solution)/shard_map/ppermute | solution.py:143
  8.9 7.7 %collective-permute-start.2 = (f32[32,512]{1,0:T(8,128)S(1)}, f32[32,512]{1,0:T(8,128)S(1)}, u32[]{:S(2)}, u32[]{:S(2)}) collective-permute-start(f32[32,512]{1,0:T(8,128)S(1)} %collective-permute-done.refs_1_), channel_id=1, source_target_pairs={{0,2},{1,3},{2,4},{3,5},{4,6},{5,7},{6,0},{7,1},{8,10},{9,11},{10,... | collective-permute-start | bytes 196616 | tf_op jit(solution)/shard_map/ppermute | solution.py:143
  11.3 0.7 %copy-start = (s32[4,2]{0,1:T(2,128)S(1)}, s32[4,2]{0,1:T(2,128)}, u32[]{:S(2)}) copy-start(s32[4,2]{0,1:T(2,128)} %param.4) | copy-start | bytes 100
  16.5 11.2 %copy-start.1 = (s32[4,2]{0,1:T(2,128)S(1)}, s32[4,2]{0,1:T(2,128)}, u32[]{:S(2)}) copy-start(s32[4,2]{0,1:T(2,128)} %param.4) | copy-start | bytes 100
  18.5 8.1 %collective-permute-start.8 = (f32[136,512]{1,0:T(8,128)S(1)}, f32[136,512]{1,0:T(8,128)S(1)}, u32[]{:S(2)}, u32[]{:S(2)}) collective-permute-start(f32[136,512]{1,0:T(8,128)S(1)} %mirror.1.own), channel_id=1, source_target_pairs={{0,16},{8,24},{16,0},{24,8},{32,48},{40,56},{48,32},{56,40},{64,80... | collective-permute-start | bytes 835592 | tf_op jit(solution)/shard_map/ppermute | solution.py:165
  21.3 24.2 %all-to-all-start = ((f32[4,2,32,512]{3,2,1,0:T(8,128)}), f32[4,2,32,512]{3,2,1,0:T(8,128)S(1)}, u32[]{:S(2)}, u32[]{:S(2)}) async-start(f32[4,2,32,512]{3,2,1,0:T(8,128)} %get-tuple-element.21), calls=%async_computation | async-start | bytes 1048576 | tf_op jit(solution)/shard_map/all_to_all | solution.py:169
  26.1 1.6 %collective-permute-start.7 = (f32[136,512]{1,0:T(8,128)S(1)}, f32[136,512]{1,0:T(8,128)S(1)}, u32[]{:S(2)}, u32[]{:S(2)}) collective-permute-start(f32[136,512]{1,0:T(8,128)S(1)} %mirror.1.own), channel_id=1, source_target_pairs={{0,8},{8,0},{16,24},{24,16},{32,40},{40,32},{48,56},{56,48},{64,72... | collective-permute-start | bytes 835592 | tf_op jit(solution)/shard_map/ppermute | solution.py:166
  26.7 1.7 %collective-permute-start.9 = (f32[136,512]{1,0:T(8,128)S(1)}, f32[136,512]{1,0:T(8,128)S(1)}, u32[]{:S(2)}, u32[]{:S(2)}) collective-permute-start(f32[136,512]{1,0:T(8,128)S(1)} %collective-permute-done.8.one), channel_id=1, source_target_pairs={{0,8},{8,0},{16,24},{24,16},{32,40},{40,32},{48,56},{56,48},{64,72... | collective-permute-start | bytes 835592 | tf_op jit(solution)/shard_map/ppermute | solution.py:167
  29.1 16.4 %collective-permute-start.10 = (f32[32,512]{1,0:T(8,128)S(1)}, f32[32,512]{1,0:T(8,128)S(1)}, u32[]{:S(2)}, u32[]{:S(2)}) collective-permute-start(f32[32,512]{1,0:T(8,128)S(1)} %get-tuple-element.24), channel_id=1, source_target_pairs={{0,64},{8,72},{16,80},{24,88},{32,96},{40,104},{48,112},{56,120},{... | collective-permute-start | bytes 196616 | tf_op jit(solution)/shard_map/ppermute | solution.py:191
  32.5 20.9 %collective-permute-start.13 = (f32[32,512]{1,0:T(8,128)S(1)}, f32[32,512]{1,0:T(8,128)S(1)}, u32[]{:S(2)}, u32[]{:S(2)}) collective-permute-start(f32[32,512]{1,0:T(8,128)S(1)} %get-tuple-element.30), channel_id=1, source_target_pairs={{0,96},{8,104},{16,112},{24,120},{32,128},{40,136},{48,144},{56,15... | collective-permute-start | bytes 196616 | tf_op jit(solution)/shard_map/ppermute | solution.py:191
  37.4 18.7 %collective-permute-start.14 = (f32[32,512]{1,0:T(8,128)S(1)}, f32[32,512]{1,0:T(8,128)S(1)}, u32[]{:S(2)}, u32[]{:S(2)}) collective-permute-start(f32[32,512]{1,0:T(8,128)S(1)} %get-tuple-element.31), channel_id=1, source_target_pairs={{0,128},{8,136},{16,144},{24,152},{32,160},{40,168},{48,176},{56,1... | collective-permute-start | bytes 196616 | tf_op jit(solution)/shard_map/ppermute | solution.py:191
  38.4 17.7 %collective-permute-start.15 = (f32[32,512]{1,0:T(8,128)S(1)}, f32[32,512]{1,0:T(8,128)S(1)}, u32[]{:S(2)}, u32[]{:S(2)}) collective-permute-start(f32[32,512]{1,0:T(8,128)S(1)} %get-tuple-element.32), channel_id=1, source_target_pairs={{0,160},{8,168},{16,176},{24,184},{32,192},{40,200},{48,208},{56,2... | collective-permute-start | bytes 196616 | tf_op jit(solution)/shard_map/ppermute | solution.py:191
  42.9 9.9 %collective-permute-start.16 = (f32[32,512]{1,0:T(8,128)S(1)}, f32[32,512]{1,0:T(8,128)S(1)}, u32[]{:S(2)}, u32[]{:S(2)}) collective-permute-start(f32[32,512]{1,0:T(8,128)S(1)} %get-tuple-element.34), channel_id=1, source_target_pairs={{0,192},{8,200},{16,208},{24,216},{32,224},{40,232},{48,240},{56,2... | collective-permute-start | bytes 196616 | tf_op jit(solution)/shard_map/ppermute | solution.py:191
  45.6 10.5 %collective-permute-start.11 = (f32[32,512]{1,0:T(8,128)S(1)}, f32[32,512]{1,0:T(8,128)S(1)}, u32[]{:S(2)}, u32[]{:S(2)}) collective-permute-start(f32[32,512]{1,0:T(8,128)S(1)} %slice_bitcast_fusion), channel_id=1, source_target_pairs={{0,1},{1,0},{2,3},{3,2},{4,5},{5,4},{6,7},{7,6},{8,9},{9,8},{10,11... | collective-permute-start | bytes 196616 | tf_op jit(solution)/shard_map/ppermute | solution.py:194
  52.8 5.5 %collective-permute-start.12 = (f32[32,512]{1,0:T(8,128)S(1)}, f32[32,512]{1,0:T(8,128)S(1)}, u32[]{:S(2)}, u32[]{:S(2)}) collective-permute-start(f32[32,512]{1,0:T(8,128)S(1)} %get-tuple-element.28), channel_id=1, source_target_pairs={{0,32},{8,40},{16,48},{24,56},{32,64},{40,72},{48,80},{56,88},{64,... | collective-permute-start | bytes 196616 | tf_op jit(solution)/shard_map/ppermute | solution.py:191
  53.4 4.9 %collective-permute-start.17 = (f32[32,512]{1,0:T(8,128)S(1)}, f32[32,512]{1,0:T(8,128)S(1)}, u32[]{:S(2)}, u32[]{:S(2)}) collective-permute-start(f32[32,512]{1,0:T(8,128)S(1)} %get-tuple-element.36), channel_id=1, source_target_pairs={{0,224},{8,232},{16,240},{24,248},{32,0},{40,8},{48,16},{56,24},{6... | collective-permute-start | bytes 196616 | tf_op jit(solution)/shard_map/ppermute | solution.py:191
